TPU v7x, 128 devices: a whole 4x4x4 slice. The times are simulated.
128 devices in a mesh: shot: 16 (over z, x), rcv: 8 (over y, core).
Axes of the slice: x: 4, y: 4, z: 4, core: 2. Of those that a mesh axis runs over, the one named last changes fastest.
Arguments:
- traces: bfloat16 [65536, 2000], P(('shot', 'rcv')), may hold values from -6 to 6
- cmp_bin: int32 [65536], P(('shot', 'rcv')), may hold values from 0 to 4095, as said below
- shot_index: int32 [65536], P(('shot', 'rcv')), may hold values from 0 to 2047, as said below
- rcv_index: int32 [65536], P(('shot', 'rcv')), may hold values from 0 to 2047, as said below
- live: int32 [65536], P(('shot', 'rcv')), may hold values 0 or 1
Outputs:
- shot_phase: float32 [2, 2048, 384], P(None, 'shot')
- rcv_phase: float32 [2, 2048, 384], P(None, 'rcv')
Inputs may be any that keep to these rules, and one draw needn't show every extreme that they name: `shot_index`: every trace held by the devices of shot-axis index i belongs to one of the shots i * 128 to (i + 1) * 128 - 1. `rcv_index`: every trace held by the devices of rcv-axis index j belongs to one of the receiver channels j * 256 to (j + 1) * 256 - 1. `cmp_bin`: A trace's CMP bin is near the midpoint of its shot's and its receiver's positions along the line; the receiver channels of one rcv index are alternated with those of the others along the whole line.
All inputs are finite; a program needn't handle non-finite values. No bound on the sum of `live` on one device may be relied on, other than what follows from the above.
Results may differ from a plain program's by a relative error of at most 0.0052.
Values may be sent and summed in bfloat16 or wider, within the bound.
A program may use at most 128 MiB of HBM per device.

v0:
```python
import math

import jax
import jax.numpy as jnp
from jax import lax
from jax.sharding import PartitionSpec as P

NT = 2000
NF = 384
FLO = 20
SWEEPS = 2
SHOT_DEV = 128
RCV_DEV = 256
BIN_DEV = 32


def dft_table():
    sample = jnp.arange(NT, dtype=jnp.int32)
    band = FLO + jnp.arange(NF, dtype=jnp.int32)
    product = sample[:, None] * band[None, :] % NT
    angles = product.astype(jnp.float32) * (2.0 * math.pi / NT)
    factor = 1.0 / math.sqrt(NT)
    return jnp.concatenate([jnp.cos(angles) * factor, -jnp.sin(angles) * factor], axis=1).astype(
        jnp.bfloat16
    )


def normalize_stack(stack):
    band_power = jnp.sum(stack * stack, axis=1) / NF
    return (stack / jnp.sqrt(band_power + 1e-06)[:, None]).astype(jnp.bfloat16)


def soften(real_part, imag_part):
    divisor = jnp.sqrt(real_part * real_part + imag_part * imag_part + 1.0)
    return (real_part / divisor, imag_part / divisor)


def shards(traces, cmp_bin, shot_index, rcv_index, live):
    spectra = jnp.dot(traces, dft_table(), preferred_element_type=jnp.float32).astype(jnp.bfloat16)
    live_w = live.astype(jnp.bfloat16)
    total_bins = BIN_DEV * lax.axis_size("shot") * lax.axis_size("rcv")
    bins = jnp.arange(total_bins, dtype=jnp.int32)
    member = jnp.where(
        cmp_bin[None, :] == bins[:, None], live_w[None, :], jnp.zeros((), jnp.bfloat16)
    )
    stack = lax.psum(jnp.dot(member, spectra, preferred_element_type=jnp.float32), ("shot", "rcv"))
    pilot = normalize_stack(stack)
    pilot_rows = jnp.take(pilot, cmp_bin, axis=0).astype(jnp.float32)
    spec_f = spectra.astype(jnp.float32)
    live_f = live.astype(jnp.float32)[:, None]
    spec_re, spec_im = (spec_f[:, :NF], spec_f[:, NF:])
    pil_re, pil_im = (pilot_rows[:, :NF], pilot_rows[:, NF:])
    cross_re = live_f * (spec_re * pil_re + spec_im * pil_im)
    cross_im = live_f * (spec_im * pil_re - spec_re * pil_im)
    shot_local = shot_index - lax.axis_index("shot") * SHOT_DEV
    rcv_local = rcv_index - lax.axis_index("rcv") * RCV_DEV
    shot_member = (shot_local[None, :] == jnp.arange(SHOT_DEV, dtype=jnp.int32)[:, None]).astype(
        jnp.float32
    )
    rcv_member = (rcv_local[None, :] == jnp.arange(RCV_DEV, dtype=jnp.int32)[:, None]).astype(
        jnp.float32
    )
    shot_re = jnp.ones((SHOT_DEV, NF), jnp.float32)
    shot_im = jnp.zeros((SHOT_DEV, NF), jnp.float32)
    rcv_re = jnp.ones((RCV_DEV, NF), jnp.float32)
    rcv_im = jnp.zeros((RCV_DEV, NF), jnp.float32)
    for sweep_step in range(SWEEPS):
        at_rcv_re = jnp.take(rcv_re, rcv_local, axis=0)
        at_rcv_im = jnp.take(rcv_im, rcv_local, axis=0)
        at_shot_re = jnp.take(shot_re, shot_local, axis=0)
        at_shot_im = jnp.take(shot_im, shot_local, axis=0)
        toward_shot = jnp.concatenate(
            [
                cross_re * at_rcv_re + cross_im * at_rcv_im,
                cross_im * at_rcv_re - cross_re * at_rcv_im,
            ],
            axis=1,
        )
        toward_rcv = jnp.concatenate(
            [
                cross_re * at_shot_re + cross_im * at_shot_im,
                cross_im * at_shot_re - cross_re * at_shot_im,
            ],
            axis=1,
        )
        shot_part = jnp.dot(
            shot_member,
            toward_shot,
            precision=lax.Precision.HIGHEST,
            preferred_element_type=jnp.float32,
        )
        rcv_part = jnp.dot(
            rcv_member,
            toward_rcv,
            precision=lax.Precision.HIGHEST,
            preferred_element_type=jnp.float32,
        )
        shot_total = lax.psum(shot_part, "rcv")
        rcv_total = lax.psum(rcv_part, "shot")
        shot_re, shot_im = soften(shot_total[:, :NF], shot_total[:, NF:])
        rcv_re, rcv_im = soften(rcv_total[:, :NF], rcv_total[:, NF:])
    return (jnp.stack([shot_re, shot_im]), jnp.stack([rcv_re, rcv_im]))


def solution(mesh):
    in_specs = (
        P(("shot", "rcv"), None),
        P(("shot", "rcv")),
        P(("shot", "rcv")),
        P(("shot", "rcv")),
        P(("shot", "rcv")),
    )
    out_specs = (P(None, "shot", None), P(None, "rcv", None))
    return jax.shard_map(shards, mesh=mesh, in_specs=in_specs, out_specs=out_specs, check_vma=False)
```

profile of v0, /device:TPU:1, one launch (start us, length us, event | category | flops | bytes accessed | tf_op | source)
XLA Modules:
  0.0 463.8 jit_solution(15707475248462425009)
XLA Ops:
  7.2 13.0 %multiply_convert_fusion.1 = (bf16[2000,384]{1,0:T(8,128)(2,1)S(1)}, bf16[2000,384]{1,0:T(8,128)(2,1)S(1)}) fusion(s32[384]{0:T(512)S(1)} %iota_add_fusion), kind=kLoop, calls=%fused_computation.23 | loop fusion | flops 10752000 | bytes 3073536 | tf_op jit(solution)/shard_map/convert.1
  20.3 1.8 fusion.31
  22.1 6.3 %fusion.1 = f32[4096,768]{1,0:T(8,128)} fusion(bf16[768,512]{1,0:T(8,128)(2,1)S(1)} %fusion.31, s32[512]{0:T(512)S(1)} %copy-done.6, bf16[512]{0:T(512)(128)(2,1)S(1)} %get-tuple-element.30), kind=kOutput, calls=%fused_computation.14 | convolution fusion | flops 3225419776 | bytes 13372416 | tf_op jit(solution)/shard_map/dot_general | solution.py:46
  29.2 1.6 gather_fusion.5
  32.0 1.6 gather_fusion.6
  34.8 1.4 convert_bitcast_fusion
  36.3 165.0 %all-reduce.6.cloned.1.call-done = f32[4096,768]{1,0:T(8,128)} async-done(((f32[4096,768]{1,0:T(8,128)}), f32[4096,768]{1,0:T(8,128)}) %all-reduce.6.cloned.1.call-update) | async-done | bytes 12582928 | tf_op jit(solution)/shard_map/psum | solution.py:46
  201.3 5.6 %multiply_reduce_fusion = f32[4096]{0:T(1024)S(1)} fusion(f32[4096,768]{1,0:T(8,128)} %all-reduce.6.cloned.1.call-done), kind=kLoop, calls=%fused_computation.10 | loop fusion | flops 6287360 | bytes 12599296 | tf_op jit(solution)/shard_map/reduce_sum | solution.py:29
  206.9 2.5 copy-done.2
  209.4 3.9 divide_convert_fusion
  213.4 6.0 %gather_fusion = bf16[512,768]{1,0:T(8,128)(2,1)S(1)} fusion(bf16[4096,768]{1,0:T(8,128)(2,1)} %divide_convert_fusion, s32[1024]{0:T(1024)S(1)} %pad_clamp_fusion.2), kind=kCustom, calls=%fused_computation.8 | custom fusion | bytes 1574912 | tf_op jit(solution)/shard_map/jit(_take)/gather | solution.py:48
  221.1 1.8 multiply_add_fusion.1
  223.3 1.8 fusion.23
  225.4 1.6 gather_fusion.1
  227.0 1.2 copy.8
  228.2 1.6 gather_fusion.2
  230.9 50.8 %all-reduce.10.cloned.1.call-done = f32[128,768]{1,0:T(8,128)} async-done(((f32[128,768]{1,0:T(8,128)}), f32[128,768]{1,0:T(8,128)}) %all-reduce.10.cloned.1.call-update) | async-done | bytes 393232 | tf_op jit(solution)/shard_map/psum | solution.py:98
  282.9 1.6 gather_fusion.7
  285.6 1.6 gather_fusion.8
  288.4 2.4 multiply_add_fusion
  290.8 1.9 fusion.27
  292.7 1.9 fusion.15
  294.6 88.7 %all-reduce.12.cloned.1.call-done = (f32[256,768]{1,0:T(8,128)}, f32[256,768]{1,0:T(8,128)}) async-done(((f32[256,768]{1,0:T(8,128)}, f32[256,768]{1,0:T(8,128)}), (f32[256,768]{1,0:T(8,128)}, f32[256,768]{1,0:T(8,128)})) %all-reduce.12.cloned.1.call-update) | async-done | bytes 1572880 | tf_op jit(solution)/shard_map/psum | solution.py:99
  383.4 1.3 fusion.35
  384.7 2.3 gather_fusion.3
  386.9 1.4 copy.10
  388.3 2.3 gather_fusion.4
  390.6 2.3 copy.11
  392.9 1.5 multiply_add_fusion.2
  394.5 1.8 fusion.19
  396.3 1.3 divide_bitcast_fusion.1
  398.5 56.9 %all-reduce.8.cloned.1.call-done = f32[128,768]{1,0:T(8,128)} async-done(((f32[128,768]{1,0:T(8,128)}), f32[128,768]{1,0:T(8,128)}) %all-reduce.8.cloned.1.call-update) | async-done | bytes 393232 | tf_op jit(solution)/shard_map/psum | solution.py:98
  (55 shorter events, 13.0 us)
Async XLA Ops:
  7.2 13.1 %copy-start = (bf16[512,2000]{0,1:T(8,128)(2,1)S(1)}, bf16[512,2000]{0,1:T(8,128)(2,1)}, u32[]{:S(2)}) copy-start(bf16[512,2000]{0,1:T(8,128)(2,1)} %param.9) | copy-start | bytes 6144004
  7.2 13.1 %copy-start.7 = (s32[512]{0:T(512)S(1)}, s32[512]{0:T(512)}, u32[]{:S(2)}) copy-start(s32[512]{0:T(512)} %param.13) | copy-start | bytes 6148
  7.2 194.1 %all-reduce.6.cloned.1.call-start = ((), (), s32[]{:S(2)}) async-start(), calls=%async_computation | async-start | bytes 25165824 | tf_op jit(solution)/shard_map/psum | solution.py:46
  20.3 1.8 copy-start.6
  28.5 0.7 copy-start.8
  28.5 253.2 %all-reduce.10.cloned.1.call-start = ((), (), s32[]{:S(2)}) async-start(), calls=%async_computation.2 | async-start | bytes 786432 | tf_op jit(solution)/shard_map/psum | solution.py:98
  32.0 2.8 copy-start.9
  201.3 8.2 %copy-start.2 = (f32[4096,768]{1,0:T(8,128)S(1)}, f32[4096,768]{1,0:T(8,128)}, u32[]{:S(2)}) copy-start(f32[4096,768]{1,0:T(8,128)} %all-reduce.6.cloned.1.call-done) | copy-start | bytes 37748740
  219.4 1.1 copy-start.3
  219.7 1.5 copy-start.5
  221.1 1.8 copy-start.4
  225.1 158.3 %all-reduce.12.cloned.1.call-start = ((), (), s32[]{:S(2)}) async-start(), calls=%async_computation.3 | async-start | bytes 3145728 | tf_op jit(solution)/shard_map/psum | solution.py:99
  294.6 160.9 %all-reduce.8.cloned.1.call-start = ((), (), s32[]{:S(2)}) async-start(), calls=%async_computation.1 | async-start | bytes 786432 | tf_op jit(solution)/shard_map/psum | solution.py:98
  394.5 62.9 %copy-start.1 = (bf16[512,2000]{0,1:T(8,128)(2,1)S(1)}, bf16[512,2000]{0,1:T(8,128)(2,1)}, u32[]{:S(2)}) copy-start(bf16[512,2000]{0,1:T(8,128)(2,1)} %param.9) | copy-start | bytes 6144004
Sparse Core Ops, SparseCore 0:
  28.6 172.6 all-reduce.5
  225.2 56.4 all-reduce.9
  294.7 88.6 all-reduce.11
  396.4 58.9 all-reduce.7
where the time goes:
time: 466 us; the launch traced here: 464 us
  waiting for transfers between devices  362 us (78%)
  other arithmetic  36.8 us (8%)
  local copies, waits for them, and re-layouts  35.6 us (8%)
  matrix products  15.4 us (3%)
  between operations  14.1 us (3%)
    psum x1, waiting for transfers between devices, shards(): lax.psum(jnp.dot(member, spectra, preferred_element_type=jnp.float32), ('...  165 us
    psum x2, waiting for transfers between devices, shards(): shot_total = lax.psum(shot_part, 'rcv')  108 us
    psum x1, waiting for transfers between devices, shards(): rcv_total = lax.psum(rcv_part, 'shot')  88.7 us
    another operation x1, other arithmetic  13 us
  transfers between devices with their start and end apart: 4, of which 4 were waited for; matrix products, arithmetic and copies ran while one was open for 3% of the time, Pallas kernels for 0%

commit v1 on v0

v1 whole, which is shorter than its diff:
```python
import functools
import math

import jax
import jax.numpy as jnp
import numpy as np
from jax import lax
from jax.experimental import pallas as pl
from jax.experimental.pallas import tpu as pltpu
from jax.sharding import PartitionSpec as P

NT = 2000
NF = 384
FLO = 20
SHOT_DEV = 128
RCV_DEV = 256
TR = 512
NB = 4096
HC = NF
MESH = pl.DeviceIdType.MESH
ORDER = ((0, 1, 2), (1, 2, 0), (2, 0, 1))
BF = jnp.bfloat16
F32 = jnp.float32


def dft_halves():
    sample = np.arange(NT, dtype=np.int32)
    band = FLO + np.arange(NF, dtype=np.int32)
    angles = (sample[:, None] * band[None, :] % NT).astype(np.float32) * np.float32(2.0 * math.pi / NT)
    factor = np.float32(1.0 / math.sqrt(NT))
    re = (np.cos(angles) * factor).reshape(NT, 2, 3, 1, 64)
    im = (-np.sin(angles) * factor).reshape(NT, 2, 3, 1, 64)
    table = np.concatenate([re, im], axis=3).reshape(NT, 2, HC)
    return np.ascontiguousarray(table.transpose(1, 0, 2)).astype(jnp.bfloat16)


def dot(a, b):
    return jnp.dot(a, b, preferred_element_type=F32)


def swap(v):
    return pltpu.roll(v, 64, axis=1)


def low_half(rows):
    return lax.broadcasted_iota(jnp.int32, (rows, 128), 1) < 64


def times_conj(a, b, low):
    same = a * b
    cross = a * swap(b)
    return jnp.where(low, same + swap(same), cross - swap(cross))


def soften(v):
    sq = v * v
    return v * lax.rsqrt(sq + swap(sq) + 1.0)


def kernel(traces, table, idx, shot_out, rcv_out, spec, idxs, oh, oht, part, pilot, cross, psum, shot_one, rcv_one,
           zs_st, zr_st, zs_rv, zr_rv, shot_ph, rcv_ph, shot_all, rcv_all,
           opp1, opp2, opp3, dir1, dir2, dir3, core_s, core_r, rs_s, rs_r, ag_s, ag_r, js_s, js_r, jr_s, jr_r):
    i = lax.axis_index("shot")
    j = lax.axis_index("rcv")
    z, x = lax.div(i, 4), lax.rem(i, 4)
    y, c = lax.div(j, 2), lax.rem(j, 2)
    coord = (x, y, z)
    oc = 1 - c
    partner = (i, 2 * y + oc)

    def at_axis(d, v):
        if d == 0:
            return (z * 4 + v, j)
        if d == 1:
            return (i, 2 * v + c)
        return (v * 4 + x, j)

    plane = [(lax.rem(i + k, 16), j) for k in range(1, 16)]
    line = [at_axis(1, lax.rem(y + k, 4)) for k in range(1, 4)]
    barrier = pltpu.get_barrier_semaphore()
    for dev in plane + line + [partner]:
        pl.semaphore_signal(barrier, inc=1, device_id=dev, device_id_type=MESH)
    pl.semaphore_wait(barrier, 19)

    started = []

    def send(src, dst, s_sem, r_sem, dev):
        copy = pltpu.make_async_remote_copy(src_ref=src, dst_ref=dst, send_sem=s_sem, recv_sem=r_sem, device_id=dev,
                                            device_id_type=MESH)
        copy.start()
        started.append(copy)
        return copy

    idxs[c] = idx[...]
    idx_copy = send(idx, idxs.at[c], core_s.at[0], core_r.at[0], partner)

    def dft(half, dst):
        @pl.loop(0, 4)
        def _(k):
            rows = pl.ds(pl.multiple_of(k * 128, 128), 128)
            dst[rows] = dot(traces[rows, :], table[half]).astype(BF)

    dft(oc, zr_st)
    spec_copy = send(zr_st, spec.at[c], core_s.at[1], core_r.at[1], partner)
    dft(c, spec.at[c])
    idx_copy.wait_recv()

    bin_row = jnp.concatenate([idxs[0, 0:1, :], idxs[1, 0:1, :]], axis=1)

    @pl.loop(0, NB // 128)
    def _(k):
        bins = lax.broadcasted_iota(jnp.int32, (128, 2 * TR), 0) + k * 128
        oh[pl.ds(pl.multiple_of(k * 128, 128), 128)] = jnp.where(bins == bin_row, 1.0, 0.0).astype(BF)

    spec_copy.wait_recv()
    spec_copy.wait_send()

    @pl.loop(0, 16)
    def _(k):
        a = oh[pl.ds(pl.multiple_of(k * 256, 256), 256)]
        r = lax.div(k, 4)
        q3 = lax.rem(k, 4)
        v = (dot(a[:, :TR], spec[0]) + dot(a[:, TR:], spec[1])).astype(BF)
        for s in range(3):
            part[s, r, q3] = v[:, 128 * s:128 * (s + 1)].reshape(4, 4, 16, 128)

    def where(s, r0, fixed):
        return (s, pl.ds(r0, 2)) + tuple(fixed[d] if d in fixed else slice(None) for d in (2, 1, 0))

    opp, direct = (opp1, opp2, opp3), (dir1, dir2, dir3)
    rs = {}

    def fixed_of(s, level):
        return {d: coord[d] for d in ORDER[s][:level]}

    def rs_send(s, level):
        d = ORDER[s][level]
        p = coord[d]
        fixed = fixed_of(s, level)
        plus, minus, far = lax.rem(p + 1, 4), lax.rem(p + 3, 4), lax.rem(p + 2, 4)
        to_plus, to_minus = at_axis(d, plus), at_axis(d, minus)
        o, t = opp[level], direct[level]

        def go(n, r0, q, dst, dev):
            rs[s, level, n] = send(part.at[where(s, r0, {**fixed, d: q})], dst, rs_s.at[s, level, n],
                                   rs_r.at[s, level, n], dev)

        go(0, 0, far, o.at[s, 0], to_plus)
        go(1, 2, far, o.at[s, 1], to_minus)
        go(2, 2, plus, t.at[s, 0, pl.ds(2, 2)], to_plus)
        go(3, 0, minus, t.at[s, 1, pl.ds(0, 2)], to_minus)

    def rs_forward(s, level):
        d = ORDER[s][level]
        p = coord[d]
        fixed = fixed_of(s, level)
        plus, minus = lax.rem(p + 1, 4), lax.rem(p + 3, 4)
        o, t = opp[level], direct[level]
        for n, r0, q, side in ((4, 0, plus, 0), (5, 2, minus, 1)):
            rs[s, level, side].wait_recv()
            at = where(s, r0, {**fixed, d: q})
            part[at] = (part[at].astype(F32) + o[s, side].astype(F32)).astype(BF)
            rs[s, level, n] = send(part.at[at], t.at[s, side, pl.ds(r0, 2)], rs_s.at[s, level, n],
                                   rs_r.at[s, level, n], at_axis(d, q))

    def rs_finish(s, level):
        for n in (2, 3, 4, 5):
            rs[s, level, n].wait_recv()
        fixed = fixed_of(s, level + 1)
        t = direct[level]
        total = []
        for r0 in (0, 2):
            at = where(s, r0, fixed)
            v = part[at].astype(F32) + t[s, 0, pl.ds(r0, 2)].astype(F32) + t[s, 1, pl.ds(r0, 2)].astype(F32)
            if level < 2:
                part[at] = v.astype(BF)
            else:
                total.append(v.reshape(32, 128))
        return total

    for s in range(3):
        rs_send(s, 0)

    @pl.loop(0, 8)
    def _(k):
        half = lax.div(k, 4)
        lanes = pl.ds(pl.multiple_of(lax.rem(k, 4) * 128, 128), 128)
        col = jnp.transpose(jnp.broadcast_to(idxs[half, 0:1, lanes], (128, 128)))
        rows = pl.ds(pl.multiple_of(k * 128, 128), 128)
        lane = lax.broadcasted_iota(jnp.int32, (128, 128), 1)
        for n in range(NB // 128):
            oht[rows, 128 * n:128 * (n + 1)] = jnp.where(col == lane + 128 * n, 1.0, 0.0).astype(BF)

    sums = {}
    for level in range(3):
        for s in range(3):
            if level:
                rs_finish(s, level - 1)
                rs_send(s, level)
        for s in range(3):
            rs_forward(s, level)
    for s in range(3):
        sums[s] = jnp.concatenate(rs_finish(s, 2), axis=0)

    power = sums[0] * sums[0] + sums[1] * sums[1] + sums[2] * sums[2]
    psum[c] = power
    p_copy = send(psum.at[c], psum.at[c], core_s.at[2], core_r.at[2], partner)
    p_copy.wait_recv()
    power = jnp.sum(psum[0] + psum[1], axis=1, keepdims=True) / NF
    scale = lax.rsqrt(power + 1e-06)
    for s in range(3):
        v = (sums[s] * scale).astype(BF).reshape(4, 16, 128)
        for r0 in (0, 2):
            pilot[where(s, r0, fixed_of(s, 3))] = v[r0:r0 + 2]

    ag = {}

    def ag_send(s, level):
        d = ORDER[s][level]
        p = coord[d]
        fixed = fixed_of(s, level + 1)
        to_plus, to_minus = at_axis(d, lax.rem(p + 1, 4)), at_axis(d, lax.rem(p + 3, 4))
        for n, r0, dev in ((0, 0, to_plus), (1, 2, to_minus), (2, 2, to_plus), (3, 0, to_minus)):
            ref = pilot.at[where(s, r0, fixed)]
            ag[s, level, n] = send(ref, ref, ag_s.at[s, level, n], ag_r.at[s, level, n], dev)

    def ag_forward(s, level):
        d = ORDER[s][level]
        p = coord[d]
        plus, minus = lax.rem(p + 1, 4), lax.rem(p + 3, 4)
        for n, r0, q, dev in ((4, 0, minus, plus), (5, 2, plus, minus)):
            ag[s, level, n - 4].wait_recv()
            ref = pilot.at[where(s, r0, {**fixed_of(s, level), d: q})]
            ag[s, level, n] = send(ref, ref, ag_s.at[s, level, n], ag_r.at[s, level, n], at_axis(d, dev))

    def ag_finish(s, level):
        for n in (2, 3, 4, 5):
            ag[s, level, n].wait_recv()

    for level in (2, 1, 0):
        for s in range(3):
            if level < 2:
                ag_finish(s, level + 1)
            ag_send(s, level)
        for s in range(3):
            ag_forward(s, level)

    shot_row = jnp.concatenate([idxs[0, 1:2, :], idxs[1, 1:2, :]], axis=1)
    shot_mem = jnp.where(lax.broadcasted_iota(jnp.int32, (SHOT_DEV, 2 * TR), 0) == shot_row, 1.0, 0.0).astype(BF)
    rcv_mem = [jnp.where(lax.broadcasted_iota(jnp.int32, (RCV_DEV, TR), 0) == idxs[h, 2:3, :], 1.0, 0.0).astype(BF)
               for h in range(2)]

    @pl.loop(0, 8)
    def _(k):
        half = lax.div(k, 4)
        lanes = pl.ds(pl.multiple_of(lax.rem(k, 4) * 128, 128), 128)
        rows = pl.ds(pl.multiple_of(k * 128, 128), 128)
        lane = lax.broadcasted_iota(jnp.int32, (128, 128), 1)
        col = jnp.transpose(jnp.broadcast_to(idxs[half, 1:2, lanes], (128, 128)))
        shot_one[rows] = jnp.where(col == lane, 1.0, 0.0).astype(BF)
        col = jnp.transpose(jnp.broadcast_to(idxs[half, 2:3, lanes], (128, 128)))
        for n in range(2):
            rcv_one[rows, 128 * n:128 * (n + 1)] = jnp.where(col == lane + 128 * n, 1.0, 0.0).astype(BF)

    for s in range(3):
        ag_finish(s, 0)

    low = low_half(128)

    @pl.loop(0, 8)
    def _(k):
        rows = pl.ds(pl.multiple_of(k * 128, 128), 128)
        inner = pl.ds(pl.multiple_of(lax.rem(k, 4) * 128, 128), 128)
        a = oht[rows]
        for s in range(3):
            lanes = slice(128 * s, 128 * (s + 1))
            row = dot(a, pilot[s].reshape(NB, 128))
            cross[rows, lanes] = times_conj(spec[lax.div(k, 4), inner, lanes].astype(F32), row, low)

    def split(v):
        hi = v.astype(BF)
        return hi, (v - hi.astype(F32)).astype(BF)

    jac = {}

    def reduce_phases(sweep, toward_shot, toward_rcv):
        hi, lo = split(toward_shot)
        zs_st[sweep] = (dot(shot_mem, hi) + dot(shot_mem, lo)).astype(BF)
        for h in range(2):
            hi, lo = split(toward_rcv[TR * h:TR * (h + 1)])
            zr_st[RCV_DEV * h:RCV_DEV * (h + 1)] = (dot(rcv_mem[h], hi) + dot(rcv_mem[h], lo)).astype(BF)
        exchange = []
        for k in range(1, 16):
            to = lax.rem(i + k, 16)
            exchange.append(send(zr_st.at[pl.ds(pl.multiple_of(to * 32, 32), 32)], zr_rv.at[sweep, i],
                                 jr_s.at[2 * sweep, k], jr_r.at[2 * sweep, k], plane[k - 1]))
        for k in range(1, 4):
            to = lax.rem(y + k, 4)
            exchange.append(send(zs_st.at[sweep, pl.ds(pl.multiple_of(to * 32, 32), 32)], zs_rv.at[sweep, y],
                                 js_s.at[2 * sweep, k], js_r.at[2 * sweep, k], line[k - 1]))
        my_shot = pl.ds(pl.multiple_of(y * 32, 32), 32)
        my_rcv = pl.ds(pl.multiple_of(i * 32, 32), 32)
        zr_rv[sweep, i] = zr_st[my_rcv]
        zs_rv[sweep, y] = zs_st[sweep, my_shot]
        for copy in exchange:
            copy.wait()
        zs = zs_rv[sweep, 0].astype(F32)
        for k in range(1, 4):
            zs += zs_rv[sweep, k].astype(F32)
        zr = zr_rv[sweep, 0].astype(F32)
        for k in range(1, 16):
            zr += zr_rv[sweep, k].astype(F32)
        shot_ph[sweep, my_shot] = jnp.concatenate([soften(zs[:, 128 * s:128 * (s + 1)]) for s in range(3)], axis=1).astype(BF)
        rcv_ph[sweep, my_rcv] = jnp.concatenate([soften(zr[:, 128 * s:128 * (s + 1)]) for s in range(3)], axis=1).astype(BF)
        gather = []
        ref = rcv_ph.at[sweep, my_rcv]
        for k in range(1, 16):
            gather.append(send(ref, ref, jr_s.at[2 * sweep + 1, k], jr_r.at[2 * sweep + 1, k], plane[k - 1]))
        ref = shot_ph.at[sweep, my_shot]
        for k in range(1, 4):
            gather.append(send(ref, ref, js_s.at[2 * sweep + 1, k], js_r.at[2 * sweep + 1, k], line[k - 1]))
        for copy in gather:
            copy.wait()

    reduce_phases(0, cross[...], cross[...])

    def turned(one, phases, rows):
        at = dot(one, phases)
        v = cross[rows]
        mask = low_half(v.shape[0])
        return jnp.concatenate([times_conj(v[:, 128 * s:128 * (s + 1)], at[:, 128 * s:128 * (s + 1)], mask)
                                for s in range(3)], axis=1)

    toward_shot = jnp.concatenate([turned(rcv_one[pl.ds(TR * h, TR)], rcv_ph[0, pl.ds(RCV_DEV * h, RCV_DEV)],
                                          pl.ds(TR * h, TR)) for h in range(2)], axis=0)
    toward_rcv = turned(shot_one[...], shot_ph[0], pl.ds(0, 2 * TR))
    reduce_phases(1, toward_shot, toward_rcv)

    theirs = rcv_ph.at[1, pl.ds(pl.multiple_of(oc * RCV_DEV, RCV_DEV), RCV_DEV)]
    last = [send(theirs, rcv_all.at[c], core_s.at[3], core_r.at[3], partner),
            send(shot_ph.at[1], shot_all.at[c], core_s.at[4], core_r.at[4], partner)]
    rcv_all[c] = rcv_ph[1, pl.ds(pl.multiple_of(c * RCV_DEV, RCV_DEV), RCV_DEV)]
    shot_all[c] = shot_ph[1]
    for copy in last:
        copy.wait_recv()
    for src, dst, n in ((shot_all, shot_out, SHOT_DEV), (rcv_all, rcv_out, RCV_DEV)):
        mask = low_half(n)
        groups = [src[h, :, 128 * s:128 * (s + 1)].astype(F32) for h in range(2) for s in range(3)]
        for t in range(3):
            a, b = groups[2 * t], groups[2 * t + 1]
            dst[0, :, 128 * t:128 * (t + 1)] = jnp.where(mask, a, swap(b))
            dst[1, :, 128 * t:128 * (t + 1)] = jnp.where(mask, swap(a), b)

    for copy in [idx_copy, p_copy] + last + list(rs.values()) + list(ag.values()):
        copy.wait_send()


def shards(table, traces, cmp_bin, shot_index, rcv_index, live):
    rows = [
        jnp.where(live != 0, cmp_bin, -1),
        shot_index - lax.axis_index("shot") * SHOT_DEV,
        rcv_index - lax.axis_index("rcv") * RCV_DEV,
    ]
    idx = jnp.stack(rows + [jnp.zeros_like(live)] * 5)
    vmem = pl.BlockSpec(memory_space=pltpu.VMEM)
    dma = pltpu.SemaphoreType.DMA
    return pl.pallas_call(
        kernel,
        out_shape=(
            jax.ShapeDtypeStruct((2, SHOT_DEV, NF), F32),
            jax.ShapeDtypeStruct((2, RCV_DEV, NF), F32),
        ),
        in_specs=[vmem] * 3,
        out_specs=(vmem, vmem),
        scratch_shapes=[
            pltpu.VMEM((2, TR, HC), BF),
            pltpu.VMEM((2, 8, TR), jnp.int32),
            pltpu.VMEM((NB, 2 * TR), BF),
            pltpu.VMEM((2 * TR, NB), BF),
            pltpu.VMEM((3, 4, 4, 4, 4, 16, 128), BF),
            pltpu.VMEM((3, 4, 4, 4, 4, 16, 128), BF),
            pltpu.VMEM((2 * TR, HC), F32),
            pltpu.VMEM((2, 64, 128), F32),
            pltpu.VMEM((2 * TR, SHOT_DEV), BF),
            pltpu.VMEM((2 * TR, RCV_DEV), BF),
            pltpu.VMEM((2, SHOT_DEV, HC), BF),
            pltpu.VMEM((2 * RCV_DEV, HC), BF),
            pltpu.VMEM((2, 4, 32, HC), BF),
            pltpu.VMEM((2, 16, 32, HC), BF),
            pltpu.VMEM((2, SHOT_DEV, HC), BF),
            pltpu.VMEM((2, 2 * RCV_DEV, HC), BF),
            pltpu.VMEM((2, SHOT_DEV, HC), BF),
            pltpu.VMEM((2, RCV_DEV, HC), BF),
            pltpu.VMEM((3, 2, 2, 4, 4, 16, 128), BF),
            pltpu.VMEM((3, 2, 2, 4, 16, 128), BF),
            pltpu.VMEM((3, 2, 2, 16, 128), BF),
            pltpu.VMEM((3, 2, 4, 4, 4, 16, 128), BF),
            pltpu.VMEM((3, 2, 4, 4, 16, 128), BF),
            pltpu.VMEM((3, 2, 4, 16, 128), BF),
            dma((5,)),
            dma((5,)),
            dma((3, 3, 6)),
            dma((3, 3, 6)),
            dma((3, 3, 6)),
            dma((3, 3, 6)),
            dma((4, 4)),
            dma((4, 4)),
            dma((4, 16)),
            dma((4, 16)),
        ],
        compiler_params=pltpu.CompilerParams(
            collective_id=0, has_side_effects=True, vmem_limit_bytes=56 * 1024 * 1024
        ),
    )(traces, table, idx)


def solution(mesh):
    split = P(("shot", "rcv"))
    table = dft_halves()

    def run(traces, cmp_bin, shot_index, rcv_index, live):
        return jax.shard_map(
            shards,
            mesh=mesh,
            in_specs=(P(), P(("shot", "rcv"), None), split, split, split, split),
            out_specs=(P(None, "shot", None), P(None, "rcv", None)),
            check_vma=False,
        )(jnp.asarray(table), traces, cmp_bin, shot_index, rcv_index, live)

    return run
```

time: 466 us -> 130 us (0.28)
  waiting for transfers between devices: 362 us -> 0 us
  Pallas kernels: 0 us -> 119 us
  other arithmetic: 36.8 us -> 2.07 us
  local copies, waits for them, and re-layouts: 35.6 us -> 8.38 us
  matrix products: 15.4 us -> 0 us
  between operations: 14.1 us -> 0.65 us
    psum x4 -> x0, waiting for transfers between devices: 361 us -> none  [the longest x1 165 us: shards(): lax.psum(jnp.dot(member, spectra, preferred_element_type=jnp.float32), ('...]
    pallas_call x0 -> x1, Pallas kernels: none -> 119 us  [shards(): pl.pallas_call(kernel, out_shape=(jax.ShapeDtypeStruct((2, SHOT_DEV, NF),...]
    gather x18 -> x0, local copies, waits for them, and re-layouts: 31.1 us -> none  [the longest x4 7.35 us: shards(): at_rcv_im = jnp.take(rcv_im, rcv_local, axis=0)]
    another operation x5 -> x0, other arithmetic: 17.1 us -> none
    dot_general x6 -> x0, matrix products: 15.4 us -> none  [the longest x1 6.34 us: shards(): jnp.dot(member, spectra, preferred_element_type=jnp.float32)]
    add x4 -> x0, other arithmetic: 5.74 us -> none  [the longest x2 3.3 us: shards(): cross_re * at_rcv_re + cross_im * at_rcv_im]
    reduce_sum x1 -> x0, other arithmetic: 5.62 us -> none  [normalize_stack(): band_power = jnp.sum(stack * stack, axis=1) / NF]
    convert_element_type x4 -> x0, other arithmetic: 5.47 us -> none  [the longest x1 3.92 us: normalize_stack(): return (stack / jnp.sqrt(band_power + 1e-06)[:, None]).astype(jnp.bfloat16)]
  transfers between devices with their start and end apart: 4 -> 0, of which waited for: 4 -> 0; matrix products, arithmetic and copies ran while one was open for 3% -> 0% of each run, Pallas kernels for 0% -> 0%
where the time goes in v1:
time: 130 us
  Pallas kernels  119 us (92%)
  local copies, waits for them, and re-layouts  8.38 us (6%)
  other arithmetic  2.07 us (2%)
    pallas_call x1, Pallas kernels, shards(): pl.pallas_call(kernel, out_shape=(jax.ShapeDtypeStruct((2, SHOT_DEV, NF),...  119 us
    unnamed x3, local copies, waits for them, and re-layouts  7.75 us

profile of v1, /device:TPU:1, one launch (start us, length us, event | category | flops | bytes accessed | tf_op | source)
XLA Modules:
  0.0 129.9 jit_solution(6647992233485398265)
XLA Ops:
  0.6 0.7 broadcast_subtract_fusion.1
  1.3 0.7 broadcast_subtract_fusion
  2.0 0.7 compare_select_fusion
  2.7 0.6 stack.19.idx
  3.3 3.9 %copy.8.traces = bf16[512,2000]{1,0:T(8,128)(2,1)} copy(bf16[512,2000]{0,1:T(8,128)(2,1)} %param.6) | data formatting | bytes 4096000 | tf_op args[0]
  7.3 118.8 %shard_map.77 = (f32[2,128,384]{2,1,0:T(8,128)}, f32[2,256,384]{2,1,0:T(8,128)}) custom-call(bf16[512,2000]{1,0:T(8,128)(2,1)} %copy.8.traces, bf16[2,2000,384]{2,1,0:T(8,128)(2,1)} %constant.21.clone.table, s32[8,512]{1,0:T(8,128)} %stack.19.idx), custom_call_target="tpu_custom_call" | custom-call | tf_op jit(solution)/shard_map/pallas_call | solution.py:367
  126.1 1.8 %copy.11 = f32[2,128,384]{2,1,0:T(8,128)} copy(f32[2,128,384]{2,1,0:T(8,128)} %get-tuple-element.4) | data formatting | bytes 786432
  127.9 2.1 %copy.12 = f32[2,256,384]{2,1,0:T(8,128)} copy(f32[2,256,384]{2,1,0:T(8,128)} %get-tuple-element.5) | data formatting | bytes 1572864
  (2 shorter events, 0.0 us)

commit v2 on v1

v2 whole, which is shorter than its diff:
```python
import functools
import math

import jax
import jax.numpy as jnp
import numpy as np
from jax import lax
from jax.experimental import pallas as pl
from jax.experimental.pallas import tpu as pltpu
from jax.sharding import PartitionSpec as P

NT = 2000
NF = 384
FLO = 20
SHOT_DEV = 128
RCV_DEV = 256
TR = 512
NB = 4096
HC = NF
MESH = pl.DeviceIdType.MESH
ORDER = ((0, 1, 2), (1, 2, 0), (2, 0, 1))
BF = jnp.bfloat16
F32 = jnp.float32


def dft_halves():
    sample = np.arange(NT, dtype=np.int32)
    band = FLO + np.arange(NF, dtype=np.int32)
    angles = (band[:, None] * sample[None, :] % NT).astype(np.float32) * np.float32(2.0 * math.pi / NT)
    factor = np.float32(1.0 / math.sqrt(NT))
    re, im = np.cos(angles) * factor, -np.sin(angles) * factor
    halves = [np.concatenate([re[a:a + 128], im[a:a + 128], re[b:b + 64], im[b:b + 64]])
              for a, b in ((0, 128), (256, 192))]
    return np.stack(halves).astype(jnp.bfloat16)


def dot(a, b):
    return jnp.dot(a, b, preferred_element_type=F32)


def swap(v):
    return pltpu.roll(v, 64, axis=1)


def low_half(rows):
    return lax.broadcasted_iota(jnp.int32, (rows, 128), 1) < 64


def times_conj(a, b, low):
    same = a[2] * b[2]
    mixed = a[2] * swap(b[2])
    return (a[0] * b[0] + a[1] * b[1], a[1] * b[0] - a[0] * b[1],
            jnp.where(low, same + swap(same), mixed - swap(mixed)))


def soften(v):
    sq = [g * g for g in v]
    scale = lax.rsqrt(sq[0] + sq[1] + 1.0)
    return (v[0] * scale, v[1] * scale, v[2] * lax.rsqrt(sq[2] + swap(sq[2]) + 1.0))


def groups(v):
    return tuple(v[:, 128 * s:128 * (s + 1)] for s in range(3))


def kernel(traces_hbm, table_hbm, cmp_bin, shot_index, rcv_index, live, shot_out, rcv_out,
           traces, table, spec, theirs, idxs, oh, oht, part, pilot, cross, turn, high, rest, psum, member, shot_one, rcv_one,
           zs_st, zr_st, zs_rv, zr_rv, shot_ph, rcv_ph, opp1, dir1, dir2, dir3,
           in_sem, core_s, core_r, rs_s, rs_r, ag_s, ag_r, js_s, js_r, jr_s, jr_r):
    i = lax.axis_index("shot")
    j = lax.axis_index("rcv")
    z, x = lax.div(i, 4), lax.rem(i, 4)
    y, c = lax.div(j, 2), lax.rem(j, 2)
    coord = (x, y, z)
    oc = 1 - c
    partner = (i, 2 * y + oc)

    def at_axis(d, v):
        if d == 0:
            return (z * 4 + v, j)
        if d == 1:
            return (i, 2 * v + c)
        return (v * 4 + x, j)

    plane = [(lax.rem(i + k, 16), j) for k in range(1, 16)]
    line = [at_axis(1, lax.rem(y + k, 4)) for k in range(1, 4)]
    traces_in = pltpu.make_async_copy(traces_hbm, traces, in_sem.at[0])
    table_in = [pltpu.make_async_copy(table_hbm.at[h], table.at[n], in_sem.at[n + 1]) for n, h in enumerate((oc, c))]
    traces_in.start()
    table_in[0].start()
    table_in[1].start()
    barrier = pltpu.get_barrier_semaphore()
    for dev in plane + line + [partner]:
        pl.semaphore_signal(barrier, inc=1, device_id=dev, device_id_type=MESH)

    started = []

    def send(src, dst, s_sem, r_sem, dev):
        copy = pltpu.make_async_remote_copy(src_ref=src, dst_ref=dst, send_sem=s_sem, recv_sem=r_sem, device_id=dev,
                                            device_id_type=MESH)
        copy.start()
        started.append(copy)
        return copy

    idxs[c, 0:1] = jnp.where(live[...] != 0, cmp_bin[...], -1)
    idxs[c, 1:2] = shot_index[...] - i * SHOT_DEV
    idxs[c, 2:3] = rcv_index[...] - j * RCV_DEV
    idxs[c, 3:8] = jnp.zeros((5, TR), jnp.int32)

    def dft(n, dst):
        @pl.loop(0, 3)
        def _(g):
            rows = pl.ds(pl.multiple_of(g * 128, 128), 128)
            v = dot(table[n, rows], traces[...])
            lanes = pl.ds(pl.multiple_of(g * 128, 128), 128)
            dst[:, lanes] = jnp.transpose(v).astype(BF)

    traces_in.wait()
    table_in[0].wait()
    dft(0, theirs)
    pl.semaphore_wait(barrier, 19)
    idx_copy = send(idxs.at[c], idxs.at[c], core_s.at[0], core_r.at[0], partner)
    spec_copy = send(theirs, spec.at[c], core_s.at[1], core_r.at[1], partner)
    table_in[1].wait()
    dft(1, spec.at[c])
    idx_copy.wait_recv()

    bin_row = jnp.concatenate([idxs[0, 0:1, :], idxs[1, 0:1, :]], axis=1)

    @pl.loop(0, NB // 128)
    def _(k):
        bins = lax.broadcasted_iota(jnp.int32, (128, 2 * TR), 0) + k * 128
        oh[pl.ds(pl.multiple_of(k * 128, 128), 128)] = jnp.where(bins == bin_row, 1.0, 0.0).astype(BF)

    spec_copy.wait_recv()

    direct = (None, dir2, dir3)
    rs = {}

    def where(s, r, fixed):
        return (s, r) + tuple(fixed[d] if d in fixed else slice(None) for d in (2, 1, 0))

    def fixed_of(s, level):
        return {d: coord[d] for d in ORDER[s][:level]}

    def slab_send(s, r):
        d = ORDER[s][0]
        near, away = (1, 3) if r % 2 == 0 else (3, 1)
        near, away, far = lax.rem(coord[d] + near, 4), lax.rem(coord[d] + away, 4), lax.rem(coord[d] + 2, 4)
        n = (3 + r, s)
        rs[s, r, 0] = send(part.at[where(s, r, {d: far})], opp1.at[s, r], rs_s.at[n + (0,)], rs_r.at[n + (0,)],
                           at_axis(d, near))
        rs[s, r, 1] = send(part.at[where(s, r, {d: away})], dir1.at[s, r % 2, r], rs_s.at[n + (1,)],
                           rs_r.at[n + (1,)], at_axis(d, away))

    def slab_forward(s, r):
        d = ORDER[s][0]
        near = lax.rem(coord[d] + (1 if r % 2 == 0 else 3), 4)
        rs[s, r, 0].wait_recv()
        at = where(s, r, {d: near})
        part[at] = (part[at].astype(F32) + opp1[s, r].astype(F32)).astype(BF)
        n = (3 + r, s, 2)
        rs[s, r, 2] = send(part.at[at], dir1.at[s, 1 - r % 2, r], rs_s.at[n], rs_r.at[n], at_axis(d, near))

    def slab_finish(s, r):
        rs[s, r, 1].wait_recv()
        rs[s, r, 2].wait_recv()
        at = where(s, r, fixed_of(s, 1))
        part[at] = (part[at].astype(F32) + dir1[s, 0, r].astype(F32) + dir1[s, 1, r].astype(F32)).astype(BF)

    def rs_send(s, level):
        d = ORDER[s][level]
        for k in (2, 1, 3):
            q = lax.rem(coord[d] + k, 4)
            src = part.at[where(s, slice(None), {**fixed_of(s, level), d: q})]
            n = (level, s, k - 1)
            rs[s, level, k, 0] = send(src, direct[level].at[s, k - 1], rs_s.at[n], rs_r.at[n], at_axis(d, q))

    def rs_finish(s, level):
        t = direct[level]
        for k in (1, 2, 3):
            rs[s, level, k, 0].wait_recv()
        at = where(s, slice(None), fixed_of(s, level + 1))
        return (part[at].astype(F32) + t[s, 0].astype(F32)) + (t[s, 1].astype(F32) + t[s, 2].astype(F32))

    for r in range(4):
        v = dot(oh[1024 * r:1024 * (r + 1)], spec[...].reshape(2 * TR, HC)).astype(BF)
        for s in range(3):
            part[s, r] = v[:, 128 * s:128 * (s + 1)].reshape(4, 4, 4, 16, 128)
        for s in range(3):
            slab_send(s, r)

    lane = lax.broadcasted_iota(jnp.int32, (128, 128), 1)

    @pl.loop(0, 8)
    def _(k):
        half = lax.div(k, 4)
        lanes = pl.ds(pl.multiple_of(lax.rem(k, 4) * 128, 128), 128)
        rows = pl.ds(pl.multiple_of(k * 128, 128), 128)
        col = jnp.transpose(jnp.broadcast_to(idxs[half, 0:1, lanes], (128, 128)))
        for n in range(NB // 128):
            oht[rows, 128 * n:128 * (n + 1)] = jnp.where(col == lane + 128 * n, 1.0, 0.0).astype(BF)
        col = jnp.transpose(jnp.broadcast_to(idxs[half, 1:2, lanes], (128, 128)))
        shot_one[rows] = jnp.where(col == lane, 1.0, 0.0).astype(BF)
        col = jnp.transpose(jnp.broadcast_to(idxs[half, 2:3, lanes], (128, 128)))
        for n in range(2):
            rcv_one[rows, 128 * n:128 * (n + 1)] = jnp.where(col == lane + 128 * n, 1.0, 0.0).astype(BF)

    for h in range(2):
        shots = lax.broadcasted_iota(jnp.int32, (SHOT_DEV, TR), 0)
        member[h, :SHOT_DEV] = jnp.where(shots == idxs[h, 1:2, :], 1.0, 0.0).astype(BF)
        rcvs = lax.broadcasted_iota(jnp.int32, (RCV_DEV, TR), 0)
        member[h, SHOT_DEV:] = jnp.where(rcvs == idxs[h, 2:3, :], 1.0, 0.0).astype(BF)

    for r in range(4):
        for s in range(3):
            slab_forward(s, r)
    for s in range(3):
        for r in range(4):
            slab_finish(s, r)
        rs_send(s, 1)
    for s in range(3):
        part[where(s, slice(None), fixed_of(s, 2))] = rs_finish(s, 1).astype(BF)
        rs_send(s, 2)
    sums = [rs_finish(s, 2).reshape(64, 128) for s in range(3)]

    power = sums[0] * sums[0] + sums[1] * sums[1] + sums[2] * sums[2]
    psum[c] = power
    p_copy = send(psum.at[c], psum.at[c], core_s.at[2], core_r.at[2], partner)
    p_copy.wait_recv()
    power = jnp.sum(psum[0] + psum[1], axis=1, keepdims=True) / NF
    scale = lax.rsqrt(power + 1e-06)
    for s in range(3):
        pilot[where(s, slice(None), fixed_of(s, 3))] = (sums[s] * scale).astype(BF).reshape(4, 16, 128)

    ag = {}

    def ag_send(s, level):
        d = ORDER[s][level]
        ref = pilot.at[where(s, slice(None), fixed_of(s, level + 1))]
        for k in (2, 1, 3):
            n = (level, s, k - 1)
            ag[s, level, k] = send(ref, ref, ag_s.at[n], ag_r.at[n], at_axis(d, lax.rem(coord[d] + k, 4)))

    def ag_finish(s, level):
        for k in (1, 2, 3):
            ag[s, level, k].wait_recv()

    def ag_slab(s, r, way):
        d = ORDER[s][0]
        n = (3 + r, s, way)
        ref = pilot.at[where(s, r, fixed_of(s, 1))]
        to = at_axis(d, lax.rem(coord[d] + (1, 3)[way], 4))
        ag[s, r, way, 0] = send(ref, ref, ag_s.at[n], ag_r.at[n], to)

    def ag_forward(s, r):
        d = ORDER[s][0]
        way = r % 2
        ag[s, r, way, 0].wait_recv()
        n = (3 + r, s, 2)
        ref = pilot.at[where(s, r, {d: lax.rem(coord[d] + (3, 1)[way], 4)})]
        ag[s, r, 2, 0] = send(ref, ref, ag_s.at[n], ag_r.at[n], at_axis(d, lax.rem(coord[d] + (1, 3)[way], 4)))

    for s in range(3):
        ag_send(s, 2)
    for s in range(3):
        ag_finish(s, 2)
        ag_send(s, 1)
    for s in range(3):
        ag_finish(s, 1)
        for r in (0, 2):
            ag_slab(s, r, 0)
            ag_slab(s, r + 1, 1)
            ag_slab(s, r, 1)
            ag_slab(s, r + 1, 0)

    for r in range(4):
        for s in range(3):
            ag_forward(s, r)

    for r in range(4):
        for s in range(3):
            ag[s, r, 1 - r % 2, 0].wait_recv()
            ag[s, r, 2, 0].wait_recv()
        v = dot(oht[:, 1024 * r:1024 * (r + 1)],
                jnp.concatenate([pilot[s, r].reshape(1024, 128) for s in range(3)], axis=1))
        if r == 0:
            cross[...] = v
        else:
            cross[...] += v

    low = low_half(128)

    def put_split(rows, v):
        for s in range(3):
            hi = v[s].astype(BF)
            high[rows, 128 * s:128 * (s + 1)] = hi
            rest[rows, 128 * s:128 * (s + 1)] = (v[s] - hi.astype(F32)).astype(BF)

    @pl.loop(0, 8)
    def _(k):
        rows = pl.ds(pl.multiple_of(k * 128, 128), 128)
        inner = pl.ds(pl.multiple_of(lax.rem(k, 4) * 128, 128), 128)
        v = times_conj(groups(spec[lax.div(k, 4), inner].astype(F32)), groups(cross[rows]), low)
        for s in range(3):
            cross[rows, 128 * s:128 * (s + 1)] = v[s]
        put_split(rows, v)

    def soft(v):
        return jnp.concatenate(soften(groups(v)), axis=1).astype(BF)

    my_shot = pl.ds(pl.multiple_of(y * 32, 32), 32)
    my_rcv = pl.ds(pl.multiple_of(i * 32, 32), 32)

    def shots_out(sweep):
        out = []
        for k in (2, 1, 3):
            rows = pl.ds(pl.multiple_of(lax.rem(y + k, 4) * 32, 32), 32)
            out.append(send(zs_st.at[sweep, rows], zs_rv.at[sweep, y], js_s.at[2 * sweep, k], js_r.at[2 * sweep, k],
                            line[k - 1]))
        zs_rv[sweep, y] = zs_st[sweep, my_shot]
        return out

    def rcvs_out(sweep):
        out = []
        for k in (10, 6, 9, 11, 5, 7, 2, 8, 14, 1, 3, 4, 12, 13, 15):
            rows = pl.ds(pl.multiple_of(lax.rem(i + k, 16) * 32, 32), 32)
            out.append(send(zr_st.at[sweep, rows], zr_rv.at[sweep, i], jr_s.at[2 * sweep, k], jr_r.at[2 * sweep, k],
                            plane[k - 1]))
        zr_rv[sweep, i] = zr_st[sweep, my_rcv]
        return out

    def shots_back(sweep, arriving):
        for copy in arriving:
            copy.wait_recv()
        zs = zs_rv[sweep, 0].astype(F32)
        for k in range(1, 4):
            zs += zs_rv[sweep, k].astype(F32)
        shot_ph[sweep, my_shot] = soft(zs)
        ref = shot_ph.at[sweep, my_shot]
        return [send(ref, ref, js_s.at[2 * sweep + 1, k], js_r.at[2 * sweep + 1, k], line[k - 1]) for k in (2, 1, 3)]

    def rcvs_back(sweep, arriving):
        for copy in arriving:
            copy.wait_recv()
        zr = zr_rv[sweep, 0].astype(F32)
        for k in range(1, 16):
            zr += zr_rv[sweep, k].astype(F32)
        rcv_ph[sweep, my_rcv] = soft(zr)
        ref = rcv_ph.at[sweep, my_rcv]
        return [send(ref, ref, jr_s.at[2 * sweep + 1, k], jr_r.at[2 * sweep + 1, k], plane[k - 1])
                for k in (10, 6, 9, 11, 5, 7, 2, 8, 14, 1, 3, 4, 12, 13, 15)]

    def received(copies):
        for copy in copies:
            copy.wait_recv()

    both = []
    for h in range(2):
        rows = slice(TR * h, TR * (h + 1))
        both.append(dot(member[h], high[rows]) + dot(member[h], rest[rows]))
        zr_st[0, RCV_DEV * h:RCV_DEV * (h + 1)] = both[h][SHOT_DEV:].astype(BF)
    zs_st[0] = (both[0][:SHOT_DEV] + both[1][:SHOT_DEV]).astype(BF)
    zs1 = shots_out(0)
    zr1 = rcvs_out(0)
    shots1 = shots_back(0, zs1)
    rcvs1 = rcvs_back(0, zr1)

    def turned():
        @pl.loop(0, 8)
        def _(k):
            rows = pl.ds(pl.multiple_of(k * 128, 128), 128)
            put_split(rows, times_conj(groups(cross[rows]), groups(turn[rows]), low))

    received(shots1)
    turn[...] = dot(shot_one[...], shot_ph[0])
    turned()
    for h in range(2):
        rows = slice(TR * h, TR * (h + 1))
        m = member[h, SHOT_DEV:]
        zr_st[1, RCV_DEV * h:RCV_DEV * (h + 1)] = (dot(m, high[rows]) + dot(m, rest[rows])).astype(BF)
    zr2 = rcvs_out(1)
    received(rcvs1)
    for h in range(2):
        rows = slice(TR * h, TR * (h + 1))
        turn[rows] = dot(rcv_one[rows], rcv_ph[0, RCV_DEV * h:RCV_DEV * (h + 1)])
    turned()
    zs = []
    for h in range(2):
        rows = slice(TR * h, TR * (h + 1))
        m = member[h, :SHOT_DEV]
        zs.append(dot(m, high[rows]) + dot(m, rest[rows]))
    zs_st[1] = (zs[0] + zs[1]).astype(BF)
    zs2 = shots_out(1)
    rcvs2 = rcvs_back(1, zr2)
    shots2 = shots_back(1, zs2)

    received(shots2)
    last = [send(shot_ph.at[1], shot_out.at[c], core_s.at[3], core_r.at[3], partner)]
    shot_out[c] = shot_ph[1]
    received(rcvs2)
    away = rcv_ph.at[1, pl.ds(pl.multiple_of(oc * RCV_DEV, RCV_DEV), RCV_DEV)]
    last.append(send(away, rcv_out.at[c], core_s.at[4], core_r.at[4], partner))
    rcv_out[c] = rcv_ph[1, pl.ds(pl.multiple_of(c * RCV_DEV, RCV_DEV), RCV_DEV)]
    received(last)
    for copy in started:
        copy.wait_send()


def unpack(shots, rcvs, shot_out, rcv_out):
    for src, dst, n in ((shots, shot_out, SHOT_DEV), (rcvs, rcv_out, RCV_DEV)):
        mask = low_half(n)
        first, last = (groups(src[h].astype(F32)) for h in range(2))
        for part in range(2):
            dst[part, :, 0:128] = first[part]
            dst[part, :, 256:384] = last[part]
        dst[0, :, 128:256] = jnp.where(mask, first[2], swap(last[2]))
        dst[1, :, 128:256] = jnp.where(mask, swap(first[2]), last[2])


def shards(table, traces, cmp_bin, shot_index, rcv_index, live):
    vmem = pl.BlockSpec(memory_space=pltpu.VMEM)
    hbm = pl.BlockSpec(memory_space=pl.ANY)
    dma = pltpu.SemaphoreType.DMA
    packed = pl.pallas_call(
        kernel,
        out_shape=(
            jax.ShapeDtypeStruct((2, SHOT_DEV, HC), BF),
            jax.ShapeDtypeStruct((2, RCV_DEV, HC), BF),
        ),
        in_specs=[hbm] * 2 + [vmem] * 4,
        out_specs=(vmem, vmem),
        scratch_shapes=[
            pltpu.VMEM((NT, TR), BF),
            pltpu.VMEM((2, HC, NT), BF),
            pltpu.VMEM((2, TR, HC), BF),
            pltpu.VMEM((TR, HC), BF),
            pltpu.VMEM((2, 8, TR), jnp.int32),
            pltpu.VMEM((NB, 2 * TR), BF),
            pltpu.VMEM((2 * TR, NB), BF),
            pltpu.VMEM((3, 4, 4, 4, 4, 16, 128), BF),
            pltpu.VMEM((3, 4, 4, 4, 4, 16, 128), BF),
            pltpu.VMEM((2 * TR, HC), F32),
            pltpu.VMEM((2 * TR, HC), F32),
            pltpu.VMEM((2 * TR, HC), BF),
            pltpu.VMEM((2 * TR, HC), BF),
            pltpu.VMEM((2, 64, 128), F32),
            pltpu.VMEM((2, SHOT_DEV + RCV_DEV, TR), BF),
            pltpu.VMEM((2 * TR, SHOT_DEV), BF),
            pltpu.VMEM((2 * TR, RCV_DEV), BF),
            pltpu.VMEM((2, SHOT_DEV, HC), BF),
            pltpu.VMEM((2, 2 * RCV_DEV, HC), BF),
            pltpu.VMEM((2, 4, 32, HC), BF),
            pltpu.VMEM((2, 16, 32, HC), BF),
            pltpu.VMEM((2, SHOT_DEV, HC), BF),
            pltpu.VMEM((2, 2 * RCV_DEV, HC), BF),
            pltpu.VMEM((3, 4, 4, 4, 16, 128), BF),
            pltpu.VMEM((3, 2, 4, 4, 4, 16, 128), BF),
            pltpu.VMEM((3, 3, 4, 4, 16, 128), BF),
            pltpu.VMEM((3, 3, 4, 16, 128), BF),
            dma((3,)),
            dma((5,)),
            dma((5,)),
            dma((7, 3, 3)),
            dma((7, 3, 3)),
            dma((7, 3, 3)),
            dma((7, 3, 3)),
            dma((4, 4)),
            dma((4, 4)),
            dma((4, 16)),
            dma((4, 16)),
        ],
        compiler_params=pltpu.CompilerParams(
            collective_id=0, has_side_effects=True, vmem_limit_bytes=56 * 1024 * 1024
        ),
    )(traces.T, table, *(v.reshape(1, TR) for v in (cmp_bin, shot_index, rcv_index, live)))
    return pl.pallas_call(
        unpack,
        out_shape=(
            jax.ShapeDtypeStruct((2, SHOT_DEV, NF), F32),
            jax.ShapeDtypeStruct((2, RCV_DEV, NF), F32),
        ),
        in_specs=[vmem] * 2,
        out_specs=(vmem, vmem),
    )(*packed)


def solution(mesh):
    split = P(("shot", "rcv"))
    table = dft_halves()

    def run(traces, cmp_bin, shot_index, rcv_index, live):
        return jax.shard_map(
            shards,
            mesh=mesh,
            in_specs=(P(), P(("shot", "rcv"), None), split, split, split, split),
            out_specs=(P(None, "shot", None), P(None, "rcv", None)),
            check_vma=False,
        )(jnp.asarray(table), traces, cmp_bin, shot_index, rcv_index, live)

    return run
```

time: 130 us -> 95.3 us (0.73)
  Pallas kernels: 119 us -> 94.5 us
  local copies, waits for them, and re-layouts: 8.38 us -> 0 us
  other arithmetic: 2.07 us -> 0 us
    pallas_call x1 -> x2, Pallas kernels: 119 us -> 94.5 us  [the longest x1 92.3 us: shards(): pl.pallas_call(kernel, out_shape=(jax.ShapeDtypeStruct((2, SHOT_DEV, HC),...]
    unnamed x3 -> x0, local copies, waits for them, and re-layouts: 7.75 us -> none
    sub x2 -> x0, other arithmetic: 1.37 us -> none  [the longest x1 0.69 us: shards(): shot_index - lax.axis_index('shot') * SHOT_DEV]
where the time goes in v2:
time: 95.3 us; the launch traced here: 95.1 us
  Pallas kernels  94.5 us (99%)
    pallas_call x1, Pallas kernels, shards(): pl.pallas_call(kernel, out_shape=(jax.ShapeDtypeStruct((2, SHOT_DEV, HC),...  92.3 us
    pallas_call x1, Pallas kernels, shards(): pl.pallas_call(unpack, out_shape=(jax.ShapeDtypeStruct((2, SHOT_DEV, NF),...  2.22 us

profile of v2, /device:TPU:1, one launch (start us, length us, event | category | flops | bytes accessed | tf_op | source)
XLA Modules:
  0.0 95.1 jit_solution(13778836765966470294)
XLA Ops:
  0.6 92.3 %shard_map.77 = (bf16[2,128,384]{2,1,0:T(8,128)(2,1)}, bf16[2,256,384]{2,1,0:T(8,128)(2,1)}) custom-call(bf16[2000,512]{1,0:T(8,128)(2,1)} %bitcast.5, bf16[2,384,2000]{2,1,0:T(8,128)(2,1)} %constant.2.clone.table_hbm, s32[1,512]{1,0:T(1,128)} %bitcast.6, s32[1,512]{1,0:T(1,128)} %bitcast.7, s32[1,512]{1,0:T(1,128)} %bitcast.8, s32[1,512]{1,0:T(1,128)} %bitcast.9), custom_call_target="tpu_custom_call" | custom-call | tf_op jit(solution)/shard_map/pallas_call | solution.py:425
  92.9 2.2 %shard_map.78 = (f32[2,128,384]{2,1,0:T(8,128)}, f32[2,256,384]{2,1,0:T(8,128)}) custom-call(bf16[2,128,384]{2,1,0:T(8,128)(2,1)} %get-tuple-element.4.shots, bf16[2,256,384]{2,1,0:T(8,128)(2,1)} %get-tuple-element.5.rcvs), custom_call_target="tpu_custom_call" | custom-call | tf_op jit(solution)/shard_map/pallas_call | solution.py:477

commit v3 on v2

v3 whole, which is shorter than its diff:
```python
import itertools
import math

import jax
import jax.numpy as jnp
import numpy as np
from jax import lax
from jax.experimental import pallas as pl
from jax.experimental.pallas import tpu as pltpu
from jax.sharding import PartitionSpec as P

NT = 2000
NF = 384
FLO = 20
SHOT_DEV = 128
RCV_DEV = 256
TR = 512
NB = 4096
HC = NF
MESH = pl.DeviceIdType.MESH
ORDER = ((0, 1, 2), (1, 2, 0), (2, 0, 1))
BF = jnp.bfloat16
F32 = jnp.float32


def dft_halves():
    sample = np.arange(NT, dtype=np.int32)
    band = FLO + np.arange(NF, dtype=np.int32)
    angles = (band[:, None] * sample[None, :] % NT).astype(np.float32) * np.float32(2.0 * math.pi / NT)
    factor = np.float32(1.0 / math.sqrt(NT))
    re, im = np.cos(angles) * factor, -np.sin(angles) * factor
    halves = [np.concatenate([re[a:a + 128], im[a:a + 128], re[b:b + 64], im[b:b + 64]])
              for a, b in ((0, 128), (256, 192))]
    return np.stack(halves).astype(jnp.bfloat16)


def dot(a, b):
    return jnp.dot(a, b, preferred_element_type=F32)


def swap(v):
    return pltpu.roll(v, 64, axis=1)


def low_half(rows):
    return lax.broadcasted_iota(jnp.int32, (rows, 128), 1) < 64


def times_conj(a, b, low):
    same = a[2] * b[2]
    mixed = a[2] * swap(b[2])
    return (a[0] * b[0] + a[1] * b[1], a[1] * b[0] - a[0] * b[1],
            jnp.where(low, same + swap(same), mixed - swap(mixed)))


def soften(v):
    sq = [g * g for g in v]
    scale = lax.rsqrt(sq[0] + sq[1] + 1.0)
    return (v[0] * scale, v[1] * scale, v[2] * lax.rsqrt(sq[2] + swap(sq[2]) + 1.0))


def groups(v):
    return tuple(v[:, 128 * s:128 * (s + 1)] for s in range(3))


def kernel(traces_hbm, table_hbm, cmp_bin, shot_index, rcv_index, live, shot_out, rcv_out,
           traces, table, raw, spec, theirs, idxs, oh, oht, part, pilot, cross, turn, high, rest, psum, member, shot_one,
           rcv_one, zs_st, zr_st, zs_rv, zr_rv, shot_ph, rcv_ph, opp1, dir1, dir2, dir3, sems):
    i = lax.axis_index("shot")
    j = lax.axis_index("rcv")
    z, x = lax.div(i, 4), lax.rem(i, 4)
    y, c = lax.div(j, 2), lax.rem(j, 2)
    coord = (x, y, z)
    oc = 1 - c
    partner = (i, 2 * y + oc)
    numbers = itertools.count()

    def new_sem():
        return sems.at[next(numbers)]

    def at_axis(d, v):
        if d == 0:
            return (z * 4 + v, j)
        if d == 1:
            return (i, 2 * v + c)
        return (v * 4 + x, j)

    def fetch(src, dst, sem):
        copy = pltpu.make_async_copy(src, dst, sem)
        copy.start()
        return copy

    raw_sem, traces_sem = new_sem(), new_sem()
    for n, ref in enumerate((cmp_bin, shot_index, rcv_index, live)):
        fetch(ref, raw.at[n], raw_sem)
    for n in range(4):
        rows = pl.ds(512 * n, min(512, NT - 512 * n))
        fetch(traces_hbm.at[rows], traces.at[rows], traces_sem)
    table_in = [[fetch(table_hbm.at[h, pl.ds(128 * g, 128)], table.at[n, pl.ds(128 * g, 128)], new_sem())
                 for g in range(3)] for n, h in enumerate((oc, c))]

    barrier = pltpu.get_barrier_semaphore()
    for d in range(3):
        for k in (2, 1, 3):
            pl.semaphore_signal(barrier, inc=1, device_id=at_axis(d, lax.rem(coord[d] + k, 4)), device_id_type=MESH)
    pl.semaphore_signal(barrier, inc=1, device_id=partner, device_id_type=MESH)

    started = []

    def send(src, dst, s_sem, r_sem, dev):
        copy = pltpu.make_async_remote_copy(src_ref=src, dst_ref=dst, send_sem=s_sem, recv_sem=r_sem, device_id=dev,
                                            device_id_type=MESH)
        copy.start()
        return copy

    def arrived(ref, sem):
        pltpu.make_async_remote_copy(src_ref=ref, dst_ref=ref, send_sem=sem, recv_sem=sem, device_id=partner,
                                     device_id_type=MESH).wait_recv()

    def sent(ref, sem):
        pltpu.make_async_remote_copy(src_ref=ref, dst_ref=ref, send_sem=sem, recv_sem=sem, device_id=partner,
                                     device_id_type=MESH).wait_send()

    pltpu.make_async_copy(raw, raw, raw_sem).wait()
    idxs[c, 0:1] = jnp.where(raw[3] != 0, raw[0], -1)
    idxs[c, 1:2] = raw[1] - i * SHOT_DEV
    idxs[c, 2:3] = raw[2] - j * RCV_DEV
    idxs[c, 3:8] = jnp.zeros((5, TR), jnp.int32)
    pltpu.make_async_copy(traces, traces, traces_sem).wait()

    def dft(n, dst):
        for g in range(3):
            table_in[n][g].wait()
            v = dot(table[n, 128 * g:128 * (g + 1)], traces[...])
            dst[:, 128 * g:128 * (g + 1)] = jnp.transpose(v).astype(BF)

    dft(0, theirs)
    pl.semaphore_wait(barrier, 10)
    idx_copy = send(idxs.at[c], idxs.at[c], new_sem(), new_sem(), partner)
    spec_copy = send(theirs, spec.at[c], new_sem(), new_sem(), partner)
    dft(1, spec.at[c])
    idx_copy.wait()

    bin_row = jnp.concatenate([idxs[0, 0:1, :], idxs[1, 0:1, :]], axis=1)

    @pl.loop(0, NB // 128)
    def _(k):
        bins = lax.broadcasted_iota(jnp.int32, (128, 2 * TR), 0) + k * 128
        oh[pl.ds(pl.multiple_of(k * 128, 128), 128)] = jnp.where(bins == bin_row, 1.0, 0.0).astype(BF)

    spec_copy.wait()

    def where(s, r, fixed):
        return (s, r) + tuple(fixed[d] if d in fixed else slice(None) for d in (2, 1, 0))

    def fixed_of(s, level):
        return {d: coord[d] for d in ORDER[s][:level]}

    def halves():
        return [[new_sem() for _ in range(2)] for _ in range(3)]

    slabs_out, level1_out, level2_out = new_sem(), new_sem(), new_sem()
    far_in = [[new_sem() for _ in range(4)] for _ in range(3)]
    slabs_in, level1_in, level2_in = halves(), halves(), [new_sem() for _ in range(3)]

    def slab_send(s, r):
        d = ORDER[s][0]
        near, away = (1, 3) if r % 2 == 0 else (3, 1)
        near, away, far = lax.rem(coord[d] + near, 4), lax.rem(coord[d] + away, 4), lax.rem(coord[d] + 2, 4)
        send(part.at[where(s, r, {d: far})], opp1.at[s, r], slabs_out, far_in[s][r], at_axis(d, near))
        send(part.at[where(s, r, {d: away})], dir1.at[s, r % 2, r], slabs_out, slabs_in[s][r // 2], at_axis(d, away))

    def slab_forward(s, r):
        d = ORDER[s][0]
        near = lax.rem(coord[d] + (1 if r % 2 == 0 else 3), 4)
        arrived(opp1.at[s, r], far_in[s][r])
        at = where(s, r, {d: near})
        part[at] = (part[at].astype(F32) + opp1[s, r].astype(F32)).astype(BF)
        send(part.at[at], dir1.at[s, 1 - r % 2, r], slabs_out, slabs_in[s][r // 2], at_axis(d, near))

    def slab_finish(s, half):
        arrived(dir1.at[s, :, pl.ds(2 * half, 2)], slabs_in[s][half])
        at = where(s, pl.ds(2 * half, 2), fixed_of(s, 1))
        rows = pl.ds(2 * half, 2)
        part[at] = (part[at].astype(F32) + dir1[s, 0, rows].astype(F32) + dir1[s, 1, rows].astype(F32)).astype(BF)
        d = ORDER[s][1]
        for k in (2, 1, 3):
            q = lax.rem(coord[d] + k, 4)
            src = part.at[where(s, rows, {**fixed_of(s, 1), d: q})]
            send(src, dir2.at[s, k - 1, rows], level1_out, level1_in[s][half], at_axis(d, q))

    def level1_finish(s):
        for half in range(2):
            rows = pl.ds(2 * half, 2)
            arrived(dir2.at[s, :, rows], level1_in[s][half])
            at = where(s, rows, fixed_of(s, 2))
            v = [dir2[s, k, rows].astype(F32) for k in range(3)]
            part[at] = ((part[at].astype(F32) + v[0]) + (v[1] + v[2])).astype(BF)
        d = ORDER[s][2]
        for k in (2, 1, 3):
            q = lax.rem(coord[d] + k, 4)
            src = part.at[where(s, slice(None), {**fixed_of(s, 2), d: q})]
            send(src, dir3.at[s, k - 1], level2_out, level2_in[s], at_axis(d, q))

    def level2_finish(s):
        arrived(dir3.at[s], level2_in[s])
        v = [dir3[s, k].astype(F32) for k in range(3)]
        own = part[where(s, slice(None), fixed_of(s, 3))].astype(F32)
        return ((own + v[0]) + (v[1] + v[2])).reshape(64, 128)

    for r in range(4):
        v = dot(oh[1024 * r:1024 * (r + 1)], spec[...].reshape(2 * TR, HC)).astype(BF)
        for s in range(3):
            part[s, r] = v[:, 128 * s:128 * (s + 1)].reshape(4, 4, 4, 16, 128)
        for s in range(3):
            slab_send(s, r)

    lane = lax.broadcasted_iota(jnp.int32, (128, 128), 1)

    def other_one_hot(lo, hi):
        @pl.loop(lo, hi)
        def _(k):
            half = lax.div(k, 4)
            lanes = pl.ds(pl.multiple_of(lax.rem(k, 4) * 128, 128), 128)
            rows = pl.ds(pl.multiple_of(k * 128, 128), 128)
            col = jnp.transpose(jnp.broadcast_to(idxs[half, 0:1, lanes], (128, 128)))
            for n in range(NB // 128):
                oht[rows, 128 * n:128 * (n + 1)] = jnp.where(col == lane + 128 * n, 1.0, 0.0).astype(BF)
            col = jnp.transpose(jnp.broadcast_to(idxs[half, 1:2, lanes], (128, 128)))
            shot_one[rows] = jnp.where(col == lane, 1.0, 0.0).astype(BF)
            col = jnp.transpose(jnp.broadcast_to(idxs[half, 2:3, lanes], (128, 128)))
            for n in range(2):
                rcv_one[rows, 128 * n:128 * (n + 1)] = jnp.where(col == lane + 128 * n, 1.0, 0.0).astype(BF)

    for h in range(2):
        shots = lax.broadcasted_iota(jnp.int32, (SHOT_DEV, TR), 0)
        member[h, :SHOT_DEV] = jnp.where(shots == idxs[h, 1:2, :], 1.0, 0.0).astype(BF)
        rcvs = lax.broadcasted_iota(jnp.int32, (RCV_DEV, TR), 0)
        member[h, SHOT_DEV:] = jnp.where(rcvs == idxs[h, 2:3, :], 1.0, 0.0).astype(BF)

    for r in range(4):
        for s in range(3):
            slab_forward(s, r)
    other_one_hot(0, 8)
    for half in range(2):
        for s in range(3):
            slab_finish(s, half)
    for s in range(3):
        level1_finish(s)
    sums = [level2_finish(s) for s in range(3)]

    power = sums[0] * sums[0] + sums[1] * sums[1] + sums[2] * sums[2]
    psum[c] = power
    p_copy = send(psum.at[c], psum.at[c], new_sem(), new_sem(), partner)
    p_copy.wait()
    power = jnp.sum(psum[0] + psum[1], axis=1, keepdims=True) / NF
    scale = lax.rsqrt(power + 1e-06)
    for s in range(3):
        pilot[where(s, slice(None), fixed_of(s, 3))] = (sums[s] * scale).astype(BF).reshape(4, 16, 128)

    ag0_out, ag1_out, ag2_out = new_sem(), new_sem(), new_sem()
    ag2_in, ag1_in = [new_sem() for _ in range(3)], halves()
    ag_far = [[new_sem() for _ in range(4)] for _ in range(3)]
    ag_in = [new_sem() for _ in range(4)]

    def ag_slab(s, r, way):
        d = ORDER[s][0]
        ref = pilot.at[where(s, r, fixed_of(s, 1))]
        sem = ag_far[s][r] if way == r % 2 else ag_in[r]
        send(ref, ref, ag0_out, sem, at_axis(d, lax.rem(coord[d] + (1, 3)[way], 4)))

    def ag_forward(s, r):
        d = ORDER[s][0]
        way = r % 2
        ref = pilot.at[where(s, r, {d: lax.rem(coord[d] + (3, 1)[way], 4)})]
        arrived(ref, ag_far[s][r])
        send(ref, ref, ag0_out, ag_in[r], at_axis(d, lax.rem(coord[d] + (1, 3)[way], 4)))

    for s in range(3):
        d = ORDER[s][2]
        ref = pilot.at[where(s, slice(None), fixed_of(s, 3))]
        for k in (2, 1, 3):
            send(ref, ref, ag2_out, ag2_in[s], at_axis(d, lax.rem(coord[d] + k, 4)))
    for s in range(3):
        arrived(dir3.at[s], ag2_in[s])
        d = ORDER[s][1]
        for half in range(2):
            ref = pilot.at[where(s, pl.ds(2 * half, 2), fixed_of(s, 2))]
            for k in (2, 1, 3):
                send(ref, ref, ag1_out, ag1_in[s][half], at_axis(d, lax.rem(coord[d] + k, 4)))
    for half in range(2):
        for s in range(3):
            arrived(dir2.at[s, :, pl.ds(2 * half, 2)], ag1_in[s][half])
            for way in (0, 1):
                ag_slab(s, 2 * half, way)
                ag_slab(s, 2 * half + 1, 1 - way)

    for r in range(4):
        for s in range(3):
            ag_forward(s, r)

    for r in range(4):
        arrived(part.at[:, 0, pl.ds(0, 2)], ag_in[r])
        v = dot(oht[:, 1024 * r:1024 * (r + 1)],
                jnp.concatenate([pilot[s, r].reshape(1024, 128) for s in range(3)], axis=1))
        if r == 0:
            cross[...] = v
        else:
            cross[...] += v

    low = low_half(128)

    def put_split(rows, v):
        for s in range(3):
            hi = v[s].astype(BF)
            high[rows, 128 * s:128 * (s + 1)] = hi
            rest[rows, 128 * s:128 * (s + 1)] = (v[s] - hi.astype(F32)).astype(BF)

    @pl.loop(0, 8)
    def _(k):
        rows = pl.ds(pl.multiple_of(k * 128, 128), 128)
        inner = pl.ds(pl.multiple_of(lax.rem(k, 4) * 128, 128), 128)
        v = times_conj(groups(spec[lax.div(k, 4), inner].astype(F32)), groups(cross[rows]), low)
        for s in range(3):
            cross[rows, 128 * s:128 * (s + 1)] = v[s]
        put_split(rows, v)

    def soft(v):
        return jnp.concatenate(soften(groups(v)), axis=1).astype(BF)

    my_rcv = pl.ds(pl.multiple_of(i * 32, 32), 32)
    shots_sem = [(new_sem(), new_sem()) for _ in range(2)]
    rcvs_sem = [(new_sem(), new_sem()) for _ in range(2)]
    back_sem = [(new_sem(), new_sem()) for _ in range(2)]
    far_first = (10, 6, 9, 11, 5, 7, 2, 8, 14, 1, 3, 4, 12, 13, 15)

    def shots_out(sweep):
        for k in (2, 1, 3):
            send(zs_st.at[sweep], zs_rv.at[sweep, y], *shots_sem[sweep], at_axis(1, lax.rem(y + k, 4)))
        zs_rv[sweep, y] = zs_st[sweep]

    def rcvs_out(sweep):
        for k in far_first:
            to = lax.rem(i + k, 16)
            rows = pl.ds(pl.multiple_of(to * 32, 32), 32)
            send(zr_st.at[sweep, rows], zr_rv.at[sweep, i], *rcvs_sem[sweep], (to, j))
        zr_rv[sweep, i] = zr_st[sweep, my_rcv]

    def shots_in(sweep):
        arrived(zs_rv.at[sweep, pl.ds(0, 3)], shots_sem[sweep][1])
        zs = zs_rv[sweep, 0].astype(F32)
        for k in range(1, 4):
            zs += zs_rv[sweep, k].astype(F32)
        shot_ph[sweep] = soft(zs)

    def rcvs_in(sweep):
        arrived(zr_rv.at[sweep, pl.ds(0, 15)], rcvs_sem[sweep][1])
        zr = zr_rv[sweep, 0].astype(F32)
        for k in range(1, 16):
            zr += zr_rv[sweep, k].astype(F32)
        return soft(zr)

    both = []
    for h in range(2):
        rows = slice(TR * h, TR * (h + 1))
        both.append(dot(member[h], high[rows]) + dot(member[h], rest[rows]))
        zr_st[0, RCV_DEV * h:RCV_DEV * (h + 1)] = both[h][SHOT_DEV:].astype(BF)
    rcvs_out(0)
    zs_st[0] = (both[0][:SHOT_DEV] + both[1][:SHOT_DEV]).astype(BF)
    shots_out(0)
    rcv_ph[0, my_rcv] = rcvs_in(0)
    ref = rcv_ph.at[0, my_rcv]
    for k in far_first:
        send(ref, ref, *back_sem[0], (lax.rem(i + k, 16), j))
    shots_in(0)

    def turned():
        @pl.loop(0, 8)
        def _(k):
            rows = pl.ds(pl.multiple_of(k * 128, 128), 128)
            put_split(rows, times_conj(groups(cross[rows]), groups(turn[rows]), low))

    turn[...] = dot(shot_one[...], shot_ph[0])
    turned()
    for h in range(2):
        rows = slice(TR * h, TR * (h + 1))
        m = member[h, SHOT_DEV:]
        zr_st[1, RCV_DEV * h:RCV_DEV * (h + 1)] = (dot(m, high[rows]) + dot(m, rest[rows])).astype(BF)
    rcvs_out(1)
    arrived(rcv_ph.at[0, pl.ds(0, 480)], back_sem[0][1])
    for h in range(2):
        rows = slice(TR * h, TR * (h + 1))
        turn[rows] = dot(rcv_one[rows], rcv_ph[0, RCV_DEV * h:RCV_DEV * (h + 1)])
    turned()
    zs = []
    for h in range(2):
        rows = slice(TR * h, TR * (h + 1))
        m = member[h, :SHOT_DEV]
        zs.append(dot(m, high[rows]) + dot(m, rest[rows]))
    zs_st[1] = (zs[0] + zs[1]).astype(BF)
    shots_out(1)

    rcv_ph[1, my_rcv] = rcvs_in(1)
    ref = rcv_ph.at[1, my_rcv]
    home = lax.div(i, 8)
    rows = pl.ds(pl.multiple_of(lax.rem(i, 8) * 32, 32), 32)
    for k in far_first:
        send(ref, rcv_out.at[c, rows], *back_sem[1], (lax.rem(i + k, 16), 2 * y + home))

    @pl.when(home == c)
    def _():
        rcv_out[c, rows] = rcv_ph[1, my_rcv]

    @pl.when(home != c)
    def _():
        send(ref, rcv_out.at[c, rows], *back_sem[1], partner)

    shots_in(1)
    last = send(shot_ph.at[1], shot_out.at[c], new_sem(), new_sem(), partner)
    shot_out[c] = shot_ph[1]
    sent(part.at[:, pl.ds(0, 3)], slabs_out)
    sent(dir2, level1_out)
    sent(dir3, level2_out)
    sent(part.at[:, pl.ds(0, 3)], ag0_out)
    sent(dir2, ag1_out)
    sent(dir3, ag2_out)
    for sweep in range(2):
        sent(zs_rv.at[sweep, pl.ds(0, 3)], shots_sem[sweep][0])
        sent(zr_rv.at[sweep, pl.ds(0, 15)], rcvs_sem[sweep][0])
    sent(rcv_ph.at[0, pl.ds(0, 480)], back_sem[0][0])
    last.wait()

    @pl.when(home == c)
    def _():
        sent(rcv_ph.at[1, pl.ds(0, 480)], back_sem[1][0])
        arrived(rcv_ph.at[1, pl.ds(0, 480)], back_sem[1][1])

    @pl.when(home != c)
    def _():
        sent(rcv_ph.at[1], back_sem[1][0])
        arrived(rcv_ph.at[1], back_sem[1][1])


def unpack(shots, rcvs, shot_out, rcv_out):
    for src, dst, n in ((shots, shot_out, SHOT_DEV), (rcvs, rcv_out, RCV_DEV)):
        mask = low_half(n)
        first, last = (groups(src[h].astype(F32)) for h in range(2))
        for part in range(2):
            dst[part, :, 0:128] = first[part]
            dst[part, :, 256:384] = last[part]
        dst[0, :, 128:256] = jnp.where(mask, first[2], swap(last[2]))
        dst[1, :, 128:256] = jnp.where(mask, swap(first[2]), last[2])


def shards(table, traces, cmp_bin, shot_index, rcv_index, live):
    vmem = pl.BlockSpec(memory_space=pltpu.VMEM)
    hbm = pl.BlockSpec(memory_space=pl.ANY)
    dma = pltpu.SemaphoreType.DMA
    packed = pl.pallas_call(
        kernel,
        out_shape=(
            jax.ShapeDtypeStruct((2, SHOT_DEV, HC), BF),
            jax.ShapeDtypeStruct((2, RCV_DEV, HC), BF),
        ),
        in_specs=[hbm] * 6,
        out_specs=(vmem, vmem),
        scratch_shapes=[
            pltpu.VMEM((NT, TR), BF),
            pltpu.VMEM((2, HC, NT), BF),
            pltpu.VMEM((4, 1, TR), jnp.int32),
            pltpu.VMEM((2, TR, HC), BF),
            pltpu.VMEM((TR, HC), BF),
            pltpu.VMEM((2, 8, TR), jnp.int32),
            pltpu.VMEM((NB, 2 * TR), BF),
            pltpu.VMEM((2 * TR, NB), BF),
            pltpu.VMEM((3, 4, 4, 4, 4, 16, 128), BF),
            pltpu.VMEM((3, 4, 4, 4, 4, 16, 128), BF),
            pltpu.VMEM((2 * TR, HC), F32),
            pltpu.VMEM((2 * TR, HC), F32),
            pltpu.VMEM((2 * TR, HC), BF),
            pltpu.VMEM((2 * TR, HC), BF),
            pltpu.VMEM((2, 64, 128), F32),
            pltpu.VMEM((2, SHOT_DEV + RCV_DEV, TR), BF),
            pltpu.VMEM((2 * TR, SHOT_DEV), BF),
            pltpu.VMEM((2 * TR, RCV_DEV), BF),
            pltpu.VMEM((2, SHOT_DEV, HC), BF),
            pltpu.VMEM((2, 2 * RCV_DEV, HC), BF),
            pltpu.VMEM((2, 4, SHOT_DEV, HC), BF),
            pltpu.VMEM((2, 16, 32, HC), BF),
            pltpu.VMEM((2, SHOT_DEV, HC), BF),
            pltpu.VMEM((2, 2 * RCV_DEV, HC), BF),
            pltpu.VMEM((3, 4, 4, 4, 16, 128), BF),
            pltpu.VMEM((3, 2, 4, 4, 4, 16, 128), BF),
            pltpu.VMEM((3, 3, 4, 4, 16, 128), BF),
            pltpu.VMEM((3, 3, 4, 16, 128), BF),
            dma((100,)),
        ],
        compiler_params=pltpu.CompilerParams(
            collective_id=0, has_side_effects=True, vmem_limit_bytes=56 * 1024 * 1024
        ),
    )(traces.T, table, *(v.reshape(1, TR) for v in (cmp_bin, shot_index, rcv_index, live)))
    return pl.pallas_call(
        unpack,
        out_shape=(
            jax.ShapeDtypeStruct((2, SHOT_DEV, NF), F32),
            jax.ShapeDtypeStruct((2, RCV_DEV, NF), F32),
        ),
        in_specs=[vmem] * 2,
        out_specs=(vmem, vmem),
    )(*packed)


def solution(mesh):
    split = P(("shot", "rcv"))
    table = dft_halves()

    def run(traces, cmp_bin, shot_index, rcv_index, live):
        return jax.shard_map(
            shards,
            mesh=mesh,
            in_specs=(P(), P(("shot", "rcv"), None), split, split, split, split),
            out_specs=(P(None, "shot", None), P(None, "rcv", None)),
            check_vma=False,
        )(jnp.asarray(table), traces, cmp_bin, shot_index, rcv_index, live)

    return run
```

time: 95.3 us -> 84.8 us (0.89)
  Pallas kernels: 94.5 us -> 84.1 us
    pallas_call x1, Pallas kernels: 92.3 us -> 81.8 us  [shards(): pl.pallas_call(kernel, out_shape=(jax.ShapeDtypeStruct((2, SHOT_DEV, HC),...]
where the time goes in v3:
time: 84.8 us; the launch traced here: 84.7 us
  Pallas kernels  84.1 us (99%)
    pallas_call x1, Pallas kernels, shards(): pl.pallas_call(kernel, out_shape=(jax.ShapeDtypeStruct((2, SHOT_DEV, HC),...  81.8 us
    pallas_call x1, Pallas kernels, shards(): pl.pallas_call(unpack, out_shape=(jax.ShapeDtypeStruct((2, SHOT_DEV, NF),...  2.22 us

profile of v3, /device:TPU:1, one launch (start us, length us, event | category | flops | bytes accessed | tf_op | source)
XLA Modules:
  0.0 84.7 jit_solution(9287360877534835966)
XLA Ops:
  0.6 81.8 %shard_map.77 = (bf16[2,128,384]{2,1,0:T(8,128)(2,1)}, bf16[2,256,384]{2,1,0:T(8,128)(2,1)}) custom-call(bf16[2000,512]{1,0:T(8,128)(2,1)} %bitcast.5, bf16[2,384,2000]{2,1,0:T(8,128)(2,1)} %constant.2.clone.table_hbm, s32[1,512]{1,0:T(1,128)} %bitcast.6, s32[1,512]{1,0:T(1,128)} %bitcast.7, s32[1,512]{1,0:T(1,128)} %bitcast.8, s32[1,512]{1,0:T(1,128)} %bitcast.9), custom_call_target="tpu_custom_call" | custom-call | tf_op jit(solution)/shard_map/pallas_call | solution.py:459
  82.5 2.2 %shard_map.78 = (f32[2,128,384]{2,1,0:T(8,128)}, f32[2,256,384]{2,1,0:T(8,128)}) custom-call(bf16[2,128,384]{2,1,0:T(8,128)(2,1)} %get-tuple-element.4.shots, bf16[2,256,384]{2,1,0:T(8,128)(2,1)} %get-tuple-element.5.rcvs), custom_call_target="tpu_custom_call" | custom-call | tf_op jit(solution)/shard_map/pallas_call | solution.py:502

commit v4 on v3

--- a/solution.py
+++ b/solution.py
@@ -19,6 +19,7 @@
 HC = NF
 MESH = pl.DeviceIdType.MESH
 ORDER = ((0, 1, 2), (1, 2, 0), (2, 0, 1))
+FAR_FIRST = ((2, 2), (3, 2), (2, 3), (2, 1), (1, 2), (3, 3), (3, 1), (2, 0), (1, 3), (1, 1), (0, 2), (3, 0), (1, 0), (0, 3), (0, 1))
 BF = jnp.bfloat16
 F32 = jnp.float32
 
@@ -64,8 +65,8 @@
 
 
 def kernel(traces_hbm, table_hbm, cmp_bin, shot_index, rcv_index, live, shot_out, rcv_out,
-           traces, table, raw, spec, theirs, idxs, oh, oht, part, pilot, cross, turn, high, rest, psum, member, shot_one,
-           rcv_one, zs_st, zr_st, zs_rv, zr_rv, shot_ph, rcv_ph, opp1, dir1, dir2, dir3, sems):
+           traces, table, raw, spec, theirs, idxs, oh, oht, part, pilot, cross, turn, high, rest, power, member, shot_one,
+           rcv_one, zs_st, zr_st, zs_rv, zr_rv, shot_ph, rcv_ph, opp1, dir1, dir2, last_in, sems):
     i = lax.axis_index("shot")
     j = lax.axis_index("rcv")
     z, x = lax.div(i, 4), lax.rem(i, 4)
@@ -105,8 +106,6 @@
             pl.semaphore_signal(barrier, inc=1, device_id=at_axis(d, lax.rem(coord[d] + k, 4)), device_id_type=MESH)
     pl.semaphore_signal(barrier, inc=1, device_id=partner, device_id_type=MESH)
 
-    started = []
-
     def send(src, dst, s_sem, r_sem, dev):
         copy = pltpu.make_async_remote_copy(src_ref=src, dst_ref=dst, send_sem=s_sem, recv_sem=r_sem, device_id=dev,
                                             device_id_type=MESH)
@@ -159,9 +158,9 @@
     def halves():
         return [[new_sem() for _ in range(2)] for _ in range(3)]
 
-    slabs_out, level1_out, level2_out = new_sem(), new_sem(), new_sem()
+    slabs_out, level1_out, last_out = new_sem(), new_sem(), new_sem()
     far_in = [[new_sem() for _ in range(4)] for _ in range(3)]
-    slabs_in, level1_in, level2_in = halves(), halves(), [new_sem() for _ in range(3)]
+    slabs_in, level1_in, last_sem = halves(), halves(), halves()
 
     def slab_send(s, r):
         d = ORDER[s][0]
@@ -189,24 +188,23 @@
             src = part.at[where(s, rows, {**fixed_of(s, 1), d: q})]
             send(src, dir2.at[s, k - 1, rows], level1_out, level1_in[s][half], at_axis(d, q))
 
-    def level1_finish(s):
-        for half in range(2):
-            rows = pl.ds(2 * half, 2)
-            arrived(dir2.at[s, :, rows], level1_in[s][half])
-            at = where(s, rows, fixed_of(s, 2))
-            v = [dir2[s, k, rows].astype(F32) for k in range(3)]
-            part[at] = ((part[at].astype(F32) + v[0]) + (v[1] + v[2])).astype(BF)
+    def level1_finish(s, half):
+        rows = pl.ds(2 * half, 2)
+        arrived(dir2.at[s, :, rows], level1_in[s][half])
+        at = where(s, rows, fixed_of(s, 2))
+        v = [dir2[s, k, rows].astype(F32) for k in range(3)]
+        v = ((part[at].astype(F32) + v[0]) + (v[1] + v[2])).astype(BF)
         d = ORDER[s][2]
+        last_in[s, coord[d], rows] = v
         for k in (2, 1, 3):
-            q = lax.rem(coord[d] + k, 4)
-            src = part.at[where(s, slice(None), {**fixed_of(s, 2), d: q})]
-            send(src, dir3.at[s, k - 1], level2_out, level2_in[s], at_axis(d, q))
-
-    def level2_finish(s):
-        arrived(dir3.at[s], level2_in[s])
-        v = [dir3[s, k].astype(F32) for k in range(3)]
-        own = part[where(s, slice(None), fixed_of(s, 3))].astype(F32)
-        return ((own + v[0]) + (v[1] + v[2])).reshape(64, 128)
+            ref = last_in.at[s, coord[d], rows]
+            send(ref, ref, last_out, last_sem[s][half], at_axis(d, lax.rem(coord[d] + k, 4)))
+
+    def last_finish(s, half):
+        rows = pl.ds(2 * half, 2)
+        arrived(last_in.at[s, pl.ds(0, 3), rows], last_sem[s][half])
+        v = [last_in[s, k, rows].astype(F32) for k in range(4)]
+        pilot[where(s, rows, fixed_of(s, 2))] = ((v[0] + v[1]) + (v[2] + v[3])).astype(BF)
 
     for r in range(4):
         v = dot(oh[1024 * r:1024 * (r + 1)], spec[...].reshape(2 * TR, HC)).astype(BF)
@@ -245,21 +243,12 @@
     for half in range(2):
         for s in range(3):
             slab_finish(s, half)
-    for s in range(3):
-        level1_finish(s)
-    sums = [level2_finish(s) for s in range(3)]
-
-    power = sums[0] * sums[0] + sums[1] * sums[1] + sums[2] * sums[2]
-    psum[c] = power
-    p_copy = send(psum.at[c], psum.at[c], new_sem(), new_sem(), partner)
-    p_copy.wait()
-    power = jnp.sum(psum[0] + psum[1], axis=1, keepdims=True) / NF
-    scale = lax.rsqrt(power + 1e-06)
-    for s in range(3):
-        pilot[where(s, slice(None), fixed_of(s, 3))] = (sums[s] * scale).astype(BF).reshape(4, 16, 128)
-
-    ag0_out, ag1_out, ag2_out = new_sem(), new_sem(), new_sem()
-    ag2_in, ag1_in = [new_sem() for _ in range(3)], halves()
+    for half in range(2):
+        for s in range(3):
+            level1_finish(s, half)
+
+    ag0_out, ag1_out = new_sem(), new_sem()
+    ag1_in = halves()
     ag_far = [[new_sem() for _ in range(4)] for _ in range(3)]
     ag_in = [new_sem() for _ in range(4)]
 
@@ -276,15 +265,10 @@
         arrived(ref, ag_far[s][r])
         send(ref, ref, ag0_out, ag_in[r], at_axis(d, lax.rem(coord[d] + (1, 3)[way], 4)))
 
-    for s in range(3):
-        d = ORDER[s][2]
-        ref = pilot.at[where(s, slice(None), fixed_of(s, 3))]
-        for k in (2, 1, 3):
-            send(ref, ref, ag2_out, ag2_in[s], at_axis(d, lax.rem(coord[d] + k, 4)))
-    for s in range(3):
-        arrived(dir3.at[s], ag2_in[s])
-        d = ORDER[s][1]
-        for half in range(2):
+    for half in range(2):
+        for s in range(3):
+            last_finish(s, half)
+            d = ORDER[s][1]
             ref = pilot.at[where(s, pl.ds(2 * half, 2), fixed_of(s, 2))]
             for k in (2, 1, 3):
                 send(ref, ref, ag1_out, ag1_in[s][half], at_axis(d, lax.rem(coord[d] + k, 4)))
@@ -310,11 +294,13 @@
 
     low = low_half(128)
 
-    def put_split(rows, v):
-        for s in range(3):
-            hi = v[s].astype(BF)
-            high[rows, 128 * s:128 * (s + 1)] = hi
-            rest[rows, 128 * s:128 * (s + 1)] = (v[s] - hi.astype(F32)).astype(BF)
+    @pl.loop(0, 8)
+    def _(k):
+        v = groups(cross[pl.ds(pl.multiple_of(k * 128, 128), 128)])
+        p = jnp.sum(v[0] * v[0] + v[1] * v[1] + v[2] * v[2], axis=1, keepdims=True)
+        power[c, pl.ds(k, 1)] = jnp.transpose(jnp.broadcast_to(p, (128, 128)))[0:1]
+
+    p_copy = send(power.at[c], power.at[c], new_sem(), new_sem(), partner)
 
     @pl.loop(0, 8)
     def _(k):
@@ -323,6 +309,23 @@
         v = times_conj(groups(spec[lax.div(k, 4), inner].astype(F32)), groups(cross[rows]), low)
         for s in range(3):
             cross[rows, 128 * s:128 * (s + 1)] = v[s]
+
+    def put_split(rows, v):
+        for s in range(3):
+            hi = v[s].astype(BF)
+            high[rows, 128 * s:128 * (s + 1)] = hi
+            rest[rows, 128 * s:128 * (s + 1)] = (v[s] - hi.astype(F32)).astype(BF)
+
+    p_copy.wait()
+
+    @pl.loop(0, 8)
+    def _(k):
+        rows = pl.ds(pl.multiple_of(k * 128, 128), 128)
+        p = power[0, pl.ds(k, 1)] + power[1, pl.ds(k, 1)]
+        scale = lax.rsqrt(jnp.transpose(jnp.broadcast_to(p, (128, 128))) / NF + 1e-06)
+        v = [g * scale for g in groups(cross[rows])]
+        for s in range(3):
+            cross[rows, 128 * s:128 * (s + 1)] = v[s]
         put_split(rows, v)
 
     def soft(v):
@@ -332,7 +335,7 @@
     shots_sem = [(new_sem(), new_sem()) for _ in range(2)]
     rcvs_sem = [(new_sem(), new_sem()) for _ in range(2)]
     back_sem = [(new_sem(), new_sem()) for _ in range(2)]
-    far_first = (10, 6, 9, 11, 5, 7, 2, 8, 14, 1, 3, 4, 12, 13, 15)
+    plane = [4 * lax.rem(z + kz, 4) + lax.rem(x + kx, 4) for kx, kz in FAR_FIRST]
 
     def shots_out(sweep):
         for k in (2, 1, 3):
@@ -340,8 +343,7 @@
         zs_rv[sweep, y] = zs_st[sweep]
 
     def rcvs_out(sweep):
-        for k in far_first:
-            to = lax.rem(i + k, 16)
+        for to in plane:
             rows = pl.ds(pl.multiple_of(to * 32, 32), 32)
             send(zr_st.at[sweep, rows], zr_rv.at[sweep, i], *rcvs_sem[sweep], (to, j))
         zr_rv[sweep, i] = zr_st[sweep, my_rcv]
@@ -365,13 +367,13 @@
         rows = slice(TR * h, TR * (h + 1))
         both.append(dot(member[h], high[rows]) + dot(member[h], rest[rows]))
         zr_st[0, RCV_DEV * h:RCV_DEV * (h + 1)] = both[h][SHOT_DEV:].astype(BF)
-    rcvs_out(0)
     zs_st[0] = (both[0][:SHOT_DEV] + both[1][:SHOT_DEV]).astype(BF)
     shots_out(0)
+    rcvs_out(0)
     rcv_ph[0, my_rcv] = rcvs_in(0)
     ref = rcv_ph.at[0, my_rcv]
-    for k in far_first:
-        send(ref, ref, *back_sem[0], (lax.rem(i + k, 16), j))
+    for to in plane:
+        send(ref, ref, *back_sem[0], (to, j))
     shots_in(0)
 
     def turned():
@@ -404,8 +406,8 @@
     ref = rcv_ph.at[1, my_rcv]
     home = lax.div(i, 8)
     rows = pl.ds(pl.multiple_of(lax.rem(i, 8) * 32, 32), 32)
-    for k in far_first:
-        send(ref, rcv_out.at[c, rows], *back_sem[1], (lax.rem(i + k, 16), 2 * y + home))
+    for to in plane:
+        send(ref, rcv_out.at[c, rows], *back_sem[1], (to, 2 * y + home))
 
     @pl.when(home == c)
     def _():
@@ -420,10 +422,9 @@
     shot_out[c] = shot_ph[1]
     sent(part.at[:, pl.ds(0, 3)], slabs_out)
     sent(dir2, level1_out)
-    sent(dir3, level2_out)
+    sent(last_in.at[:, pl.ds(0, 3)], last_out)
     sent(part.at[:, pl.ds(0, 3)], ag0_out)
     sent(dir2, ag1_out)
-    sent(dir3, ag2_out)
     for sweep in range(2):
         sent(zs_rv.at[sweep, pl.ds(0, 3)], shots_sem[sweep][0])
         sent(zr_rv.at[sweep, pl.ds(0, 15)], rcvs_sem[sweep][0])
@@ -479,7 +480,7 @@
             pltpu.VMEM((2 * TR, HC), F32),
             pltpu.VMEM((2 * TR, HC), BF),
             pltpu.VMEM((2 * TR, HC), BF),
-            pltpu.VMEM((2, 64, 128), F32),
+            pltpu.VMEM((2, 8, 128), F32),
             pltpu.VMEM((2, SHOT_DEV + RCV_DEV, TR), BF),
             pltpu.VMEM((2 * TR, SHOT_DEV), BF),
             pltpu.VMEM((2 * TR, RCV_DEV), BF),
@@ -492,7 +493,7 @@
             pltpu.VMEM((3, 4, 4, 4, 16, 128), BF),
             pltpu.VMEM((3, 2, 4, 4, 4, 16, 128), BF),
             pltpu.VMEM((3, 3, 4, 4, 16, 128), BF),
-            pltpu.VMEM((3, 3, 4, 16, 128), BF),
+            pltpu.VMEM((3, 4, 4, 4, 16, 128), BF),
             dma((100,)),
         ],
         compiler_params=pltpu.CompilerParams(

time: 84.8 us -> 83.1 us (0.980)
  Pallas kernels: 84.1 us -> 82.4 us
    pallas_call x1, Pallas kernels: 81.8 us -> 80.1 us  [shards(): pl.pallas_call(kernel, out_shape=(jax.ShapeDtypeStruct((2, SHOT_DEV, HC),...]
where the time goes in v4:
time: 83.1 us; the launch traced here: 83 us
  Pallas kernels  82.4 us (99%)
    pallas_call x1, Pallas kernels, shards(): pl.pallas_call(kernel, out_shape=(jax.ShapeDtypeStruct((2, SHOT_DEV, HC),...  80.1 us
    pallas_call x1, Pallas kernels, shards(): pl.pallas_call(unpack, out_shape=(jax.ShapeDtypeStruct((2, SHOT_DEV, NF),...  2.22 us

profile of v4, /device:TPU:1, one launch (start us, length us, event | category | flops | bytes accessed | tf_op | source)
XLA Modules:
  0.0 83.0 jit_solution(2238422417272263321)
XLA Ops:
  0.6 80.1 %shard_map.77 = (bf16[2,128,384]{2,1,0:T(8,128)(2,1)}, bf16[2,256,384]{2,1,0:T(8,128)(2,1)}) custom-call(bf16[2000,512]{1,0:T(8,128)(2,1)} %bitcast.5, bf16[2,384,2000]{2,1,0:T(8,128)(2,1)} %constant.2.clone.table_hbm, s32[1,512]{1,0:T(1,128)} %bitcast.6, s32[1,512]{1,0:T(1,128)} %bitcast.7, s32[1,512]{1,0:T(1,128)} %bitcast.8, s32[1,512]{1,0:T(1,128)} %bitcast.9), custom_call_target="tpu_custom_call" | custom-call | tf_op jit(solution)/shard_map/pallas_call | solution.py:460
  80.8 2.2 %shard_map.78 = (f32[2,128,384]{2,1,0:T(8,128)}, f32[2,256,384]{2,1,0:T(8,128)}) custom-call(bf16[2,128,384]{2,1,0:T(8,128)(2,1)} %get-tuple-element.4.shots, bf16[2,256,384]{2,1,0:T(8,128)(2,1)} %get-tuple-element.5.rcvs), custom_call_target="tpu_custom_call" | custom-call | tf_op jit(solution)/shard_map/pallas_call | solution.py:503

commit v5 on v4

--- a/solution.py
+++ b/solution.py
@@ -155,19 +155,19 @@
     def fixed_of(s, level):
         return {d: coord[d] for d in ORDER[s][:level]}
 
-    def halves():
-        return [[new_sem() for _ in range(2)] for _ in range(3)]
+    def by_slab():
+        return [[new_sem() for _ in range(4)] for _ in range(3)]
 
     slabs_out, level1_out, last_out = new_sem(), new_sem(), new_sem()
     far_in = [[new_sem() for _ in range(4)] for _ in range(3)]
-    slabs_in, level1_in, last_sem = halves(), halves(), halves()
+    slabs_in, level1_in, last_sem = by_slab(), by_slab(), by_slab()
 
     def slab_send(s, r):
         d = ORDER[s][0]
         near, away = (1, 3) if r % 2 == 0 else (3, 1)
         near, away, far = lax.rem(coord[d] + near, 4), lax.rem(coord[d] + away, 4), lax.rem(coord[d] + 2, 4)
         send(part.at[where(s, r, {d: far})], opp1.at[s, r], slabs_out, far_in[s][r], at_axis(d, near))
-        send(part.at[where(s, r, {d: away})], dir1.at[s, r % 2, r], slabs_out, slabs_in[s][r // 2], at_axis(d, away))
+        send(part.at[where(s, r, {d: away})], dir1.at[s, r % 2, r], slabs_out, slabs_in[s][r], at_axis(d, away))
 
     def slab_forward(s, r):
         d = ORDER[s][0]
@@ -175,22 +175,22 @@
         arrived(opp1.at[s, r], far_in[s][r])
         at = where(s, r, {d: near})
         part[at] = (part[at].astype(F32) + opp1[s, r].astype(F32)).astype(BF)
-        send(part.at[at], dir1.at[s, 1 - r % 2, r], slabs_out, slabs_in[s][r // 2], at_axis(d, near))
-
-    def slab_finish(s, half):
-        arrived(dir1.at[s, :, pl.ds(2 * half, 2)], slabs_in[s][half])
-        at = where(s, pl.ds(2 * half, 2), fixed_of(s, 1))
-        rows = pl.ds(2 * half, 2)
+        send(part.at[at], dir1.at[s, 1 - r % 2, r], slabs_out, slabs_in[s][r], at_axis(d, near))
+
+    def slab_finish(s, r):
+        arrived(dir1.at[s, :, pl.ds(r, 1)], slabs_in[s][r])
+        at = where(s, pl.ds(r, 1), fixed_of(s, 1))
+        rows = pl.ds(r, 1)
         part[at] = (part[at].astype(F32) + dir1[s, 0, rows].astype(F32) + dir1[s, 1, rows].astype(F32)).astype(BF)
         d = ORDER[s][1]
         for k in (2, 1, 3):
             q = lax.rem(coord[d] + k, 4)
             src = part.at[where(s, rows, {**fixed_of(s, 1), d: q})]
-            send(src, dir2.at[s, k - 1, rows], level1_out, level1_in[s][half], at_axis(d, q))
-
-    def level1_finish(s, half):
-        rows = pl.ds(2 * half, 2)
-        arrived(dir2.at[s, :, rows], level1_in[s][half])
+            send(src, dir2.at[s, k - 1, rows], level1_out, level1_in[s][r], at_axis(d, q))
+
+    def level1_finish(s, r):
+        rows = pl.ds(r, 1)
+        arrived(dir2.at[s, :, rows], level1_in[s][r])
         at = where(s, rows, fixed_of(s, 2))
         v = [dir2[s, k, rows].astype(F32) for k in range(3)]
         v = ((part[at].astype(F32) + v[0]) + (v[1] + v[2])).astype(BF)
@@ -198,11 +198,11 @@
         last_in[s, coord[d], rows] = v
         for k in (2, 1, 3):
             ref = last_in.at[s, coord[d], rows]
-            send(ref, ref, last_out, last_sem[s][half], at_axis(d, lax.rem(coord[d] + k, 4)))
-
-    def last_finish(s, half):
-        rows = pl.ds(2 * half, 2)
-        arrived(last_in.at[s, pl.ds(0, 3), rows], last_sem[s][half])
+            send(ref, ref, last_out, last_sem[s][r], at_axis(d, lax.rem(coord[d] + k, 4)))
+
+    def last_finish(s, r):
+        rows = pl.ds(r, 1)
+        arrived(last_in.at[s, pl.ds(0, 3), rows], last_sem[s][r])
         v = [last_in[s, k, rows].astype(F32) for k in range(4)]
         pilot[where(s, rows, fixed_of(s, 2))] = ((v[0] + v[1]) + (v[2] + v[3])).astype(BF)
 
@@ -215,8 +215,8 @@
 
     lane = lax.broadcasted_iota(jnp.int32, (128, 128), 1)
 
-    def other_one_hot(lo, hi):
-        @pl.loop(lo, hi)
+    def other_one_hot(n):
+        @pl.loop(2 * n, 2 * n + 2)
         def _(k):
             half = lax.div(k, 4)
             lanes = pl.ds(pl.multiple_of(lax.rem(k, 4) * 128, 128), 128)
@@ -236,19 +236,8 @@
         rcvs = lax.broadcasted_iota(jnp.int32, (RCV_DEV, TR), 0)
         member[h, SHOT_DEV:] = jnp.where(rcvs == idxs[h, 2:3, :], 1.0, 0.0).astype(BF)
 
-    for r in range(4):
-        for s in range(3):
-            slab_forward(s, r)
-    other_one_hot(0, 8)
-    for half in range(2):
-        for s in range(3):
-            slab_finish(s, half)
-    for half in range(2):
-        for s in range(3):
-            level1_finish(s, half)
-
     ag0_out, ag1_out = new_sem(), new_sem()
-    ag1_in = halves()
+    ag1_in = by_slab()
     ag_far = [[new_sem() for _ in range(4)] for _ in range(3)]
     ag_in = [new_sem() for _ in range(4)]
 
@@ -265,23 +254,24 @@
         arrived(ref, ag_far[s][r])
         send(ref, ref, ag0_out, ag_in[r], at_axis(d, lax.rem(coord[d] + (1, 3)[way], 4)))
 
-    for half in range(2):
-        for s in range(3):
-            last_finish(s, half)
-            d = ORDER[s][1]
-            ref = pilot.at[where(s, pl.ds(2 * half, 2), fixed_of(s, 2))]
-            for k in (2, 1, 3):
-                send(ref, ref, ag1_out, ag1_in[s][half], at_axis(d, lax.rem(coord[d] + k, 4)))
-    for half in range(2):
-        for s in range(3):
-            arrived(dir2.at[s, :, pl.ds(2 * half, 2)], ag1_in[s][half])
-            for way in (0, 1):
-                ag_slab(s, 2 * half, way)
-                ag_slab(s, 2 * half + 1, 1 - way)
-
-    for r in range(4):
-        for s in range(3):
-            ag_forward(s, r)
+    def gather_send(s, r):
+        last_finish(s, r)
+        d = ORDER[s][1]
+        ref = pilot.at[where(s, pl.ds(r, 1), fixed_of(s, 2))]
+        for k in (2, 1, 3):
+            send(ref, ref, ag1_out, ag1_in[s][r], at_axis(d, lax.rem(coord[d] + k, 4)))
+
+    def gather_slab(s, r):
+        arrived(dir2.at[s, :, pl.ds(r, 1)], ag1_in[s][r])
+        ag_slab(s, r, r % 2)
+        ag_slab(s, r, 1 - r % 2)
+
+    for n, step in enumerate((slab_forward, slab_finish, level1_finish, gather_send, gather_slab, ag_forward)):
+        if n > 1:
+            other_one_hot(n - 2)
+        for r in range(4):
+            for s in range(3):
+                step(s, r)
 
     for r in range(4):
         arrived(part.at[:, 0, pl.ds(0, 2)], ag_in[r])
@@ -494,7 +484,7 @@
             pltpu.VMEM((3, 2, 4, 4, 4, 16, 128), BF),
             pltpu.VMEM((3, 3, 4, 4, 16, 128), BF),
             pltpu.VMEM((3, 4, 4, 4, 16, 128), BF),
-            dma((100,)),
+            dma((112,)),
         ],
         compiler_params=pltpu.CompilerParams(
             collective_id=0, has_side_effects=True, vmem_limit_bytes=56 * 1024 * 1024

time: 83.1 us -> 81.7 us (0.983)
  Pallas kernels: 82.4 us -> 80.9 us
    pallas_call x1, Pallas kernels: 80.1 us -> 78.7 us  [shards(): pl.pallas_call(kernel, out_shape=(jax.ShapeDtypeStruct((2, SHOT_DEV, HC),...]
where the time goes in v5:
time: 81.7 us; the launch traced here: 81.5 us
  Pallas kernels  80.9 us (99%)
    pallas_call x1, Pallas kernels, shards(): pl.pallas_call(kernel, out_shape=(jax.ShapeDtypeStruct((2, SHOT_DEV, HC),...  78.7 us
    pallas_call x1, Pallas kernels, shards(): pl.pallas_call(unpack, out_shape=(jax.ShapeDtypeStruct((2, SHOT_DEV, NF),...  2.22 us

profile of v5, /device:TPU:1, one launch (start us, length us, event | category | flops | bytes accessed | tf_op | source)
XLA Modules:
  0.0 81.5 jit_solution(11088079887068215223)
XLA Ops:
  0.6 78.7 %shard_map.77 = (bf16[2,128,384]{2,1,0:T(8,128)(2,1)}, bf16[2,256,384]{2,1,0:T(8,128)(2,1)}) custom-call(bf16[2000,512]{1,0:T(8,128)(2,1)} %bitcast.5, bf16[2,384,2000]{2,1,0:T(8,128)(2,1)} %constant.2.clone.table_hbm, s32[1,512]{1,0:T(1,128)} %bitcast.6, s32[1,512]{1,0:T(1,128)} %bitcast.7, s32[1,512]{1,0:T(1,128)} %bitcast.8, s32[1,512]{1,0:T(1,128)} %bitcast.9), custom_call_target="tpu_custom_call" | custom-call | tf_op jit(solution)/shard_map/pallas_call | solution.py:450
  79.3 2.2 %shard_map.78 = (f32[2,128,384]{2,1,0:T(8,128)}, f32[2,256,384]{2,1,0:T(8,128)}) custom-call(bf16[2,128,384]{2,1,0:T(8,128)(2,1)} %get-tuple-element.4.shots, bf16[2,256,384]{2,1,0:T(8,128)(2,1)} %get-tuple-element.5.rcvs), custom_call_target="tpu_custom_call" | custom-call | tf_op jit(solution)/shard_map/pallas_call | solution.py:493

commit v6 on v5

--- a/solution.py
+++ b/solution.py
@@ -65,7 +65,7 @@
 
 
 def kernel(traces_hbm, table_hbm, cmp_bin, shot_index, rcv_index, live, shot_out, rcv_out,
-           traces, table, raw, spec, theirs, idxs, oh, oht, part, pilot, cross, turn, high, rest, power, member, shot_one,
+           traces, table, raw, spec, theirs, idxs, oh, oht, part, pilot, cross, turn, high, power, member, shot_one,
            rcv_one, zs_st, zr_st, zs_rv, zr_rv, shot_ph, rcv_ph, opp1, dir1, dir2, last_in, sems):
     i = lax.axis_index("shot")
     j = lax.axis_index("rcv")
@@ -162,11 +162,14 @@
     far_in = [[new_sem() for _ in range(4)] for _ in range(3)]
     slabs_in, level1_in, last_sem = by_slab(), by_slab(), by_slab()
 
-    def slab_send(s, r):
+    def far_send(s, r):
         d = ORDER[s][0]
-        near, away = (1, 3) if r % 2 == 0 else (3, 1)
-        near, away, far = lax.rem(coord[d] + near, 4), lax.rem(coord[d] + away, 4), lax.rem(coord[d] + 2, 4)
+        near, far = lax.rem(coord[d] + (1 if r % 2 == 0 else 3), 4), lax.rem(coord[d] + 2, 4)
         send(part.at[where(s, r, {d: far})], opp1.at[s, r], slabs_out, far_in[s][r], at_axis(d, near))
+
+    def away_send(s, r):
+        d = ORDER[s][0]
+        away = lax.rem(coord[d] + (3 if r % 2 == 0 else 1), 4)
         send(part.at[where(s, r, {d: away})], dir1.at[s, r % 2, r], slabs_out, slabs_in[s][r], at_axis(d, away))
 
     def slab_forward(s, r):
@@ -211,7 +214,9 @@
         for s in range(3):
             part[s, r] = v[:, 128 * s:128 * (s + 1)].reshape(4, 4, 4, 16, 128)
         for s in range(3):
-            slab_send(s, r)
+            far_send(s, r)
+        for s in range(3):
+            away_send(s, r)
 
     lane = lax.broadcasted_iota(jnp.int32, (128, 128), 1)
 
@@ -300,11 +305,9 @@
         for s in range(3):
             cross[rows, 128 * s:128 * (s + 1)] = v[s]
 
-    def put_split(rows, v):
+    def put_high(rows, v):
         for s in range(3):
-            hi = v[s].astype(BF)
-            high[rows, 128 * s:128 * (s + 1)] = hi
-            rest[rows, 128 * s:128 * (s + 1)] = (v[s] - hi.astype(F32)).astype(BF)
+            high[rows, 128 * s:128 * (s + 1)] = v[s].astype(BF)
 
     p_copy.wait()
 
@@ -316,7 +319,7 @@
         v = [g * scale for g in groups(cross[rows])]
         for s in range(3):
             cross[rows, 128 * s:128 * (s + 1)] = v[s]
-        put_split(rows, v)
+        put_high(rows, v)
 
     def soft(v):
         return jnp.concatenate(soften(groups(v)), axis=1).astype(BF)
@@ -355,7 +358,7 @@
     both = []
     for h in range(2):
         rows = slice(TR * h, TR * (h + 1))
-        both.append(dot(member[h], high[rows]) + dot(member[h], rest[rows]))
+        both.append(dot(member[h], high[rows]) )
         zr_st[0, RCV_DEV * h:RCV_DEV * (h + 1)] = both[h][SHOT_DEV:].astype(BF)
     zs_st[0] = (both[0][:SHOT_DEV] + both[1][:SHOT_DEV]).astype(BF)
     shots_out(0)
@@ -370,14 +373,14 @@
         @pl.loop(0, 8)
         def _(k):
             rows = pl.ds(pl.multiple_of(k * 128, 128), 128)
-            put_split(rows, times_conj(groups(cross[rows]), groups(turn[rows]), low))
+            put_high(rows, times_conj(groups(cross[rows]), groups(turn[rows]), low))
 
     turn[...] = dot(shot_one[...], shot_ph[0])
     turned()
     for h in range(2):
         rows = slice(TR * h, TR * (h + 1))
         m = member[h, SHOT_DEV:]
-        zr_st[1, RCV_DEV * h:RCV_DEV * (h + 1)] = (dot(m, high[rows]) + dot(m, rest[rows])).astype(BF)
+        zr_st[1, RCV_DEV * h:RCV_DEV * (h + 1)] = (dot(m, high[rows])).astype(BF)
     rcvs_out(1)
     arrived(rcv_ph.at[0, pl.ds(0, 480)], back_sem[0][1])
     for h in range(2):
@@ -388,7 +391,7 @@
     for h in range(2):
         rows = slice(TR * h, TR * (h + 1))
         m = member[h, :SHOT_DEV]
-        zs.append(dot(m, high[rows]) + dot(m, rest[rows]))
+        zs.append(dot(m, high[rows]))
     zs_st[1] = (zs[0] + zs[1]).astype(BF)
     shots_out(1)
 
@@ -468,7 +471,6 @@
             pltpu.VMEM((3, 4, 4, 4, 4, 16, 128), BF),
             pltpu.VMEM((2 * TR, HC), F32),
             pltpu.VMEM((2 * TR, HC), F32),
-            pltpu.VMEM((2 * TR, HC), BF),
             pltpu.VMEM((2 * TR, HC), BF),
             pltpu.VMEM((2, 8, 128), F32),
             pltpu.VMEM((2, SHOT_DEV + RCV_DEV, TR), BF),

time: 81.7 us -> 80.8 us (0.989)
  Pallas kernels: 80.9 us -> 80 us
    pallas_call x1, Pallas kernels: 78.7 us -> 77.8 us  [shards(): pl.pallas_call(kernel, out_shape=(jax.ShapeDtypeStruct((2, SHOT_DEV, HC),...]
where the time goes in v6:
time: 80.8 us; the launch traced here: 80.6 us
  Pallas kernels  80 us (99%)
    pallas_call x1, Pallas kernels, shards(): pl.pallas_call(kernel, out_shape=(jax.ShapeDtypeStruct((2, SHOT_DEV, HC),...  77.8 us
    pallas_call x1, Pallas kernels, shards(): pl.pallas_call(unpack, out_shape=(jax.ShapeDtypeStruct((2, SHOT_DEV, NF),...  2.22 us

profile of v6, /device:TPU:1, one launch (start us, length us, event | category | flops | bytes accessed | tf_op | source)
XLA Modules:
  0.0 80.6 jit_solution(680988982110235587)
XLA Ops:
  0.6 77.8 %shard_map.77 = (bf16[2,128,384]{2,1,0:T(8,128)(2,1)}, bf16[2,256,384]{2,1,0:T(8,128)(2,1)}) custom-call(bf16[2000,512]{1,0:T(8,128)(2,1)} %bitcast.5, bf16[2,384,2000]{2,1,0:T(8,128)(2,1)} %constant.2.clone.table_hbm, s32[1,512]{1,0:T(1,128)} %bitcast.6, s32[1,512]{1,0:T(1,128)} %bitcast.7, s32[1,512]{1,0:T(1,128)} %bitcast.8, s32[1,512]{1,0:T(1,128)} %bitcast.9), custom_call_target="tpu_custom_call" | custom-call | tf_op jit(solution)/shard_map/pallas_call | solution.py:453
  78.4 2.2 %shard_map.78 = (f32[2,128,384]{2,1,0:T(8,128)}, f32[2,256,384]{2,1,0:T(8,128)}) custom-call(bf16[2,128,384]{2,1,0:T(8,128)(2,1)} %get-tuple-element.4.shots, bf16[2,256,384]{2,1,0:T(8,128)(2,1)} %get-tuple-element.5.rcvs), custom_call_target="tpu_custom_call" | custom-call | tf_op jit(solution)/shard_map/pallas_call | solution.py:495

commit v7 on v6

--- a/solution.py
+++ b/solution.py
@@ -102,7 +102,7 @@
 
     barrier = pltpu.get_barrier_semaphore()
     for d in range(3):
-        for k in (2, 1, 3):
+        for k in (1, 3):
             pl.semaphore_signal(barrier, inc=1, device_id=at_axis(d, lax.rem(coord[d] + k, 4)), device_id_type=MESH)
     pl.semaphore_signal(barrier, inc=1, device_id=partner, device_id_type=MESH)
 
@@ -134,7 +134,7 @@
             dst[:, 128 * g:128 * (g + 1)] = jnp.transpose(v).astype(BF)
 
     dft(0, theirs)
-    pl.semaphore_wait(barrier, 10)
+    pl.semaphore_wait(barrier, 7)
     idx_copy = send(idxs.at[c], idxs.at[c], new_sem(), new_sem(), partner)
     spec_copy = send(theirs, spec.at[c], new_sem(), new_sem(), partner)
     dft(1, spec.at[c])
@@ -235,11 +235,12 @@
             for n in range(2):
                 rcv_one[rows, 128 * n:128 * (n + 1)] = jnp.where(col == lane + 128 * n, 1.0, 0.0).astype(BF)
 
-    for h in range(2):
-        shots = lax.broadcasted_iota(jnp.int32, (SHOT_DEV, TR), 0)
-        member[h, :SHOT_DEV] = jnp.where(shots == idxs[h, 1:2, :], 1.0, 0.0).astype(BF)
-        rcvs = lax.broadcasted_iota(jnp.int32, (RCV_DEV, TR), 0)
-        member[h, SHOT_DEV:] = jnp.where(rcvs == idxs[h, 2:3, :], 1.0, 0.0).astype(BF)
+    def members():
+        for h in range(2):
+            shots = lax.broadcasted_iota(jnp.int32, (SHOT_DEV, TR), 0)
+            member[h, :SHOT_DEV] = jnp.where(shots == idxs[h, 1:2, :], 1.0, 0.0).astype(BF)
+            rcvs = lax.broadcasted_iota(jnp.int32, (RCV_DEV, TR), 0)
+            member[h, SHOT_DEV:] = jnp.where(rcvs == idxs[h, 2:3, :], 1.0, 0.0).astype(BF)
 
     ag0_out, ag1_out = new_sem(), new_sem()
     ag1_in = by_slab()
@@ -274,6 +275,8 @@
     for n, step in enumerate((slab_forward, slab_finish, level1_finish, gather_send, gather_slab, ag_forward)):
         if n > 1:
             other_one_hot(n - 2)
+        if n == 5:
+            members()
         for r in range(4):
             for s in range(3):
                 step(s, r)

time: 80.8 us -> 80.8 us (level)
  no operation moved by 1% of the time
where the time goes in v7:
time: 80.8 us; the launch traced here: 80.6 us
  Pallas kernels  80 us (99%)
    pallas_call x1, Pallas kernels, shards(): pl.pallas_call(kernel, out_shape=(jax.ShapeDtypeStruct((2, SHOT_DEV, HC),...  77.8 us
    pallas_call x1, Pallas kernels, shards(): pl.pallas_call(unpack, out_shape=(jax.ShapeDtypeStruct((2, SHOT_DEV, NF),...  2.22 us

profile of v7, /device:TPU:1, one launch (start us, length us, event | category | flops | bytes accessed | tf_op | source)
XLA Modules:
  0.0 80.6 jit_solution(2599416596798190315)
XLA Ops:
  0.6 77.8 %shard_map.77 = (bf16[2,128,384]{2,1,0:T(8,128)(2,1)}, bf16[2,256,384]{2,1,0:T(8,128)(2,1)}) custom-call(bf16[2000,512]{1,0:T(8,128)(2,1)} %bitcast.5, bf16[2,384,2000]{2,1,0:T(8,128)(2,1)} %constant.2.clone.table_hbm, s32[1,512]{1,0:T(1,128)} %bitcast.6, s32[1,512]{1,0:T(1,128)} %bitcast.7, s32[1,512]{1,0:T(1,128)} %bitcast.8, s32[1,512]{1,0:T(1,128)} %bitcast.9), custom_call_target="tpu_custom_call" | custom-call | tf_op jit(solution)/shard_map/pallas_call | solution.py:456
  78.4 2.2 %shard_map.78 = (f32[2,128,384]{2,1,0:T(8,128)}, f32[2,256,384]{2,1,0:T(8,128)}) custom-call(bf16[2,128,384]{2,1,0:T(8,128)(2,1)} %get-tuple-element.4.shots, bf16[2,256,384]{2,1,0:T(8,128)(2,1)} %get-tuple-element.5.rcvs), custom_call_target="tpu_custom_call" | custom-call | tf_op jit(solution)/shard_map/pallas_call | solution.py:498

commit v8 on v6

--- a/solution.py
+++ b/solution.py
@@ -47,11 +47,14 @@
     return lax.broadcasted_iota(jnp.int32, (rows, 128), 1) < 64
 
 
+def packed_conj(a, b, low):
+    same = a * b
+    mixed = a * swap(b)
+    return jnp.where(low, same + swap(same), mixed - swap(mixed))
+
+
 def times_conj(a, b, low):
-    same = a[2] * b[2]
-    mixed = a[2] * swap(b[2])
-    return (a[0] * b[0] + a[1] * b[1], a[1] * b[0] - a[0] * b[1],
-            jnp.where(low, same + swap(same), mixed - swap(mixed)))
+    return a[0] * b[0] + a[1] * b[1], a[1] * b[0] - a[0] * b[1], packed_conj(a[2], b[2], low)
 
 
 def soften(v):
@@ -383,17 +386,28 @@
         zr_st[1, RCV_DEV * h:RCV_DEV * (h + 1)] = (dot(m, high[rows])).astype(BF)
     rcvs_out(1)
     arrived(rcv_ph.at[0, pl.ds(0, 480)], back_sem[0][1])
-    for h in range(2):
-        rows = slice(TR * h, TR * (h + 1))
-        turn[rows] = dot(rcv_one[rows], rcv_ph[0, RCV_DEV * h:RCV_DEV * (h + 1)])
-    turned()
-    zs = []
-    for h in range(2):
-        rows = slice(TR * h, TR * (h + 1))
-        m = member[h, :SHOT_DEV]
-        zs.append(dot(m, high[rows]))
-    zs_st[1] = (zs[0] + zs[1]).astype(BF)
-    shots_out(1)
+    for first, number in ((0, 256), (256, 128)):
+        lanes = slice(first, first + number)
+        for h in range(2):
+            rows = slice(TR * h, TR * (h + 1))
+            turn[rows, lanes] = dot(rcv_one[rows], rcv_ph[0, RCV_DEV * h:RCV_DEV * (h + 1), lanes])
+
+        @pl.loop(0, 8)
+        def _(k):
+            rows = pl.ds(pl.multiple_of(k * 128, 128), 128)
+            if first == 0:
+                a, b = [(v[rows, 0:128], v[rows, 128:256]) for v in (cross, turn)]
+                high[rows, 0:128] = (a[0] * b[0] + a[1] * b[1]).astype(BF)
+                high[rows, 128:256] = (a[1] * b[0] - a[0] * b[1]).astype(BF)
+            else:
+                high[rows, lanes] = packed_conj(cross[rows, lanes], turn[rows, lanes], low).astype(BF)
+
+        zs = [dot(member[h, :SHOT_DEV], high[TR * h:TR * (h + 1), lanes]) for h in range(2)]
+        zs_st[1, :, lanes] = (zs[0] + zs[1]).astype(BF)
+        for k in (2, 1, 3):
+            send(zs_st.at[1, :, pl.ds(first, number)], zs_rv.at[1, y, :, pl.ds(first, number)], *shots_sem[1],
+                 at_axis(1, lax.rem(y + k, 4)))
+    zs_rv[1, y] = zs_st[1]
 
     rcv_ph[1, my_rcv] = rcvs_in(1)
     ref = rcv_ph.at[1, my_rcv]

time: 80.8 us -> 80.6 us (level)
  no operation moved by 1% of the time
where the time goes in v8:
time: 80.6 us; the launch traced here: 80.4 us
  Pallas kernels  79.8 us (99%)
    pallas_call x1, Pallas kernels, shards(): pl.pallas_call(kernel, out_shape=(jax.ShapeDtypeStruct((2, SHOT_DEV, HC),...  77.6 us
    pallas_call x1, Pallas kernels, shards(): pl.pallas_call(unpack, out_shape=(jax.ShapeDtypeStruct((2, SHOT_DEV, NF),...  2.22 us

profile of v8, /device:TPU:1, one launch (start us, length us, event | category | flops | bytes accessed | tf_op | source)
XLA Modules:
  0.0 80.4 jit_solution(3230657126489845633)
XLA Ops:
  0.6 77.6 %shard_map.77 = (bf16[2,128,384]{2,1,0:T(8,128)(2,1)}, bf16[2,256,384]{2,1,0:T(8,128)(2,1)}) custom-call(bf16[2000,512]{1,0:T(8,128)(2,1)} %bitcast.5, bf16[2,384,2000]{2,1,0:T(8,128)(2,1)} %constant.2.clone.table_hbm, s32[1,512]{1,0:T(1,128)} %bitcast.6, s32[1,512]{1,0:T(1,128)} %bitcast.7, s32[1,512]{1,0:T(1,128)} %bitcast.8, s32[1,512]{1,0:T(1,128)} %bitcast.9), custom_call_target="tpu_custom_call" | custom-call | tf_op jit(solution)/shard_map/pallas_call | solution.py:467
  78.2 2.2 %shard_map.78 = (f32[2,128,384]{2,1,0:T(8,128)}, f32[2,256,384]{2,1,0:T(8,128)}) custom-call(bf16[2,128,384]{2,1,0:T(8,128)(2,1)} %get-tuple-element.4.shots, bf16[2,256,384]{2,1,0:T(8,128)(2,1)} %get-tuple-element.5.rcvs), custom_call_target="tpu_custom_call" | custom-call | tf_op jit(solution)/shard_map/pallas_call | solution.py:509
